TPU v7x, 32 devices: a whole 2x2x4 slice. The times are simulated.
32 devices in a mesh: row: 4 (over x, core), col: 8 (over z, y).
Axes of the slice: x: 2, y: 2, z: 4, core: 2. Of those that a mesh axis runs over, the one named last changes fastest.
Arguments:
- block_in: bfloat16 [4096, 2048], P('col', 'row'), may hold values from -6 to 6
- cotangent: bfloat16 [4096, 2048], P('col', 'row'), may hold values from -6 to 6
- segments: int32 [4096], P('row'), may hold values from 0 to 31, never falling along the last dimension, each value on 1 to 1024 neighbouring positions
- w_query: bfloat16 [2048, 2048], P('row', 'col'), may hold values from -0.125 to 0.125
- w_key: bfloat16 [2048, 2048], P('row', 'col'), may hold values from -0.125 to 0.125
- w_value: bfloat16 [2048, 4096], P('row', 'col'), may hold values from -0.125 to 0.125
- w_gate: bfloat16 [2048, 4096], P('row', 'col'), may hold values from -0.125 to 0.125
- w_out: bfloat16 [4096, 2048], P('col', 'row'), may hold values from -0.09375 to 0.09375
- w_up: bfloat16 [2048, 4096], P('row', 'col'), may hold values from -0.125 to 0.125
- w_down: bfloat16 [4096, 2048], P('col', 'row'), may hold values from -0.09375 to 0.09375
- retention_norm_gain: float32 [2048], P('row'), may hold values from 0.25 to 1.75
- retention_norm_bias: float32 [2048], P('row'), may hold values from -3 to 3
- feedforward_norm_gain: float32 [2048], P('row'), may hold values from 0.25 to 1.75
- feedforward_norm_bias: float32 [2048], P('row'), may hold values from -3 to 3
Outputs:
- block_out: bfloat16 [4096, 2048], P('col', 'row')
- grad_in: float32 [4096, 2048], P('col', 'row')
- grad_query: float32 [2048, 2048], P('row', 'col')
- grad_key: float32 [2048, 2048], P('row', 'col')
- grad_value: float32 [2048, 4096], P('row', 'col')
- grad_gate: float32 [2048, 4096], P('row', 'col')
- grad_out: float32 [4096, 2048], P('col', 'row')
- grad_up: float32 [2048, 4096], P('row', 'col')
- grad_down: float32 [4096, 2048], P('col', 'row')
- grad_attn_gain: float32 [2048], P('row')
- grad_attn_bias: float32 [2048], P('row')
- grad_ffn_gain: float32 [2048], P('row')
- grad_ffn_bias: float32 [2048], P('row')
Inputs may be any that keep to these rules, and one draw needn't show every extreme that they name: `segments`: segment numbers never fall along the tokens; a document holds 1 to 1024 tokens.
All inputs are finite; a program needn't handle non-finite values.
Results may differ from a plain program's by a relative error of at most 0.014.
The roundings to bfloat16 on the way count: a program that leaves them out, or rounds other values in their place, can miss the bound.
Values may be sent and summed in bfloat16 or wider, within the bound.
No kernel may reach another device: no remote copies, remote signals or barrier semaphores. Data moves between devices by JAX's collectives and lax.ppermute only.
A program may use at most 320 MiB of HBM per device.

v0:
```python
import jax
import jax.numpy as jnp
from jax import lax
from jax.sharding import Mesh
from jax.sharding import PartitionSpec as P

HEADS = 8
EPS_NORM = 1e-05
EPS_GROUP = 0.25
ROW = ("x", "k")
GROUP = ("x", "k", "y")
EVERY = ("x", "k", "z", "y")
F32 = jnp.float32
BF16 = jnp.bfloat16


def dot(left, right, over):
    return lax.dot_general(left, right, (over, ((), ())), preferred_element_type=F32)


def swap(value, mask):
    return lax.ppermute(value, GROUP, [(i, i ^ mask) for i in range(8)])


def group_gather(part):
    near = jnp.stack([part, swap(part, 1), swap(part, 4), swap(part, 5)])
    near = near.reshape((2, 1, 2) + part.shape)
    return jnp.concatenate([near, swap(near, 2)], axis=1).reshape((-1,) + part.shape[1:])


def group_reduce(total):
    blocks = total.reshape(2, 2, 2, total.shape[0] // 8, total.shape[1])
    pair = (blocks[:, 0] + swap(blocks[:, 1].astype(BF16), 2).astype(F32)).astype(BF16)
    own = pair[0, 0].astype(F32)
    for i, j in ((0, 1), (1, 0), (1, 1)):
        own = own + swap(pair[i, j], 4 * i + j).astype(F32)
    return own


def row_exchange(parts):
    return lax.all_to_all(parts, ROW, split_axis=0, concat_axis=0, tiled=True)


def to_tokens(part):
    tokens, width = part.shape
    moved = row_exchange(part.reshape(4, tokens // 4, width))
    return moved.transpose(1, 0, 2).reshape(tokens // 4, 4 * width)


def from_tokens(part):
    tokens, width = part.shape
    moved = row_exchange(part.reshape(tokens, 4, width // 4).transpose(1, 0, 2))
    return moved.reshape(4 * tokens, width // 4)


def head_order(count):
    units = count // HEADS
    j = lax.iota(jnp.int32, count)
    target = j % HEADS * units + j // HEADS
    return (target[:, None] == lax.iota(jnp.int32, count)[None, :]).astype(BF16)


def layernorm(value, gain, bias):
    mean = jnp.mean(value, axis=1, keepdims=True)
    centered = value - mean
    inverse = lax.rsqrt(jnp.mean(centered * centered, axis=1, keepdims=True) + EPS_NORM)
    hat = centered * inverse
    return (hat, inverse, (hat * gain + bias).astype(BF16))


def layernorm_back(grad, hat, inverse, gain):
    scaled = grad * gain
    first = jnp.mean(scaled, axis=1, keepdims=True)
    second = jnp.mean(scaled * hat, axis=1, keepdims=True)
    return (
        inverse * (scaled - first - hat * second),
        jnp.sum(grad * hat, axis=0),
        jnp.sum(grad, axis=0),
    )


def gelu_exact(value):
    return jax.nn.gelu(value, approximate=False)


def body(
    block_in,
    cotangent,
    segments,
    w_query,
    w_key,
    w_value,
    w_gate,
    w_out,
    w_up,
    w_down,
    retention_norm_gain,
    retention_norm_bias,
    feedforward_norm_gain,
    feedforward_norm_bias,
):
    depth = lax.axis_size("z")
    part = block_in.shape[1]
    width = 4 * part
    own = lax.axis_index(GROUP)
    plane = lax.axis_index("z")
    tokens = block_in.shape[0] // 4
    seq = 8 * tokens
    kq = w_query.shape[1] // HEADS
    kv = w_value.shape[1] // HEADS
    order_q = head_order(w_query.shape[1])
    order_v = head_order(w_value.shape[1])

    def by_head(weight, order):
        return dot(order, weight, ((0,), (1,))).astype(BF16).reshape(HEADS, -1, part)

    send_qkv = jnp.concatenate(
        [by_head(w_query, order_q), by_head(w_key, order_q), by_head(w_value, order_v)], axis=1
    )
    send_go = jnp.concatenate(
        [
            by_head(w_gate, order_v),
            dot(order_v, w_out, ((0,), (0,))).astype(BF16).reshape(HEADS, -1, part),
        ],
        axis=1,
    )

    def to_heads(send):
        got = lax.all_to_all(send, GROUP, split_axis=0, concat_axis=0, tiled=True)
        got = got.reshape(4, 2, send.shape[1], part).transpose(1, 2, 0, 3)
        return got.reshape(2, send.shape[1], width)

    got_qkv = to_heads(send_qkv)
    got_go = to_heads(send_go)
    mine_qkv = jnp.concatenate(
        [
            got_qkv[:, :kq].reshape(2 * kq, width),
            got_qkv[:, kq : 2 * kq].reshape(2 * kq, width),
            got_qkv[:, 2 * kq :].reshape(2 * kv, width),
        ],
        axis=0,
    )
    mine_go = jnp.concatenate(
        [got_go[:, :kv].reshape(2 * kv, width), got_go[:, kv:].reshape(2 * kv, width)], axis=0
    )

    def to_units(weight):
        got = row_exchange(weight.reshape(4, -1, part))
        return got.transpose(1, 0, 2).reshape(-1, width)

    mine_up = to_units(w_up.T)
    mine_down = to_units(w_down)

    def planes(mine):
        return lax.all_gather(mine, "z", axis=0, tiled=True)

    all_qkv = planes(mine_qkv)
    all_go = planes(mine_go).reshape(depth, 4 * kv, width)
    wt_gate = all_go[:, : 2 * kv].reshape(-1, width)
    wt_out = all_go[:, 2 * kv :].reshape(-1, width)
    wt_up = planes(mine_up)
    wt_down = planes(mine_down)
    params = lax.all_gather(
        jnp.stack(
            [retention_norm_gain, retention_norm_bias, feedforward_norm_gain, feedforward_norm_bias]
        ),
        ROW,
        axis=1,
        tiled=True,
    )
    stream = to_tokens(block_in).astype(F32)
    cot_own = to_tokens(cotangent)
    hat_one, inv_one, norm_one = layernorm(stream, params[0], params[1])
    x_one = group_gather(norm_one)
    cot = group_gather(cot_own)
    segs = lax.all_gather(segments, ROW, axis=0, tiled=True).reshape(depth, 8, tokens)
    ids = lax.iota(jnp.int32, 8) ^ own
    ids = ids % 2 * 4 + ids // 2
    picked = (ids[:, None] == lax.iota(jnp.int32, 8)[None, :])[:, :, None]
    here = (lax.iota(jnp.int32, depth) == plane)[:, None, None]
    seg_plane = jnp.sum(jnp.where(here, segs, 0), axis=0)
    seg = jnp.sum(jnp.where(picked, seg_plane[None], 0), axis=1).reshape(seq)
    pos = (ids[:, None] * tokens + lax.iota(jnp.int32, tokens)[None, :]).reshape(seq)
    loggam = jnp.log1p(-jnp.exp2(-5.0 - own.astype(F32)))
    gap = pos[:, None] - pos[None, :]
    inside = (gap >= 0) & (seg[:, None] == seg[None, :])
    decay = jnp.where(inside, jnp.exp(jnp.maximum(gap, 0).astype(F32) * loggam), F32(0.0))
    scale = (kq * 2 * depth) ** (-0.5)
    qkv = dot(all_qkv, x_one, ((1,), (1,))).astype(BF16).reshape(depth, -1, seq)
    query = qkv[:, : 2 * kq].reshape(-1, seq)
    keys = qkv[:, 2 * kq : 4 * kq].reshape(-1, seq)
    values = qkv[:, 4 * kq :].reshape(-1, seq)
    raw = dot(query, keys, ((0,), (0,)))
    weights = (raw * scale * decay).astype(BF16)
    retained = dot(values, weights, ((1,), (1,)))
    centered = retained - jnp.mean(retained, axis=0, keepdims=True)
    inv_group = lax.rsqrt(jnp.mean(centered * centered, axis=0, keepdims=True) + EPS_GROUP)
    normed = centered * inv_group
    normed_low = normed.astype(BF16).astype(F32)
    gate = dot(wt_gate, x_one, ((1,), (1,)))
    sigma = jax.nn.sigmoid(gate)
    swish = gate * sigma
    hidden = (swish * normed_low).astype(BF16)
    middle = stream + group_reduce(dot(hidden, wt_out, ((0,), (0,))))
    hat_two, inv_two, norm_two = layernorm(middle, params[2], params[3])
    x_two = group_gather(norm_two)
    pre = dot(wt_up, x_two, ((1,), (1,)))
    act_wide, act_pull = jax.vjp(gelu_exact, pre)
    act = act_wide.astype(BF16)
    grad_act = dot(wt_down, cot, ((1,), (1,)))
    grad_pre = act_pull(grad_act)[0].astype(BF16)
    grad_two = group_reduce(dot(grad_pre, wt_up, ((0,), (0,))))
    ffn = group_reduce(dot(act, wt_down, ((0,), (0,))))
    block_out = from_tokens((middle + ffn).astype(BF16))

    def home(full):
        return lax.psum_scatter(full.astype(BF16), "z", scatter_dimension=0, tiled=True)

    def from_units(mine):
        send = mine.reshape(-1, 4, part).transpose(1, 0, 2)
        return row_exchange(send).reshape(-1, part)

    grad_down = from_units(home(dot(act, cot, ((1,), (0,))))).astype(F32)
    grad_up = from_units(home(dot(grad_pre, x_two, ((1,), (0,))))).T.astype(F32)
    back_two, grad_ffn_gain, grad_ffn_bias = layernorm_back(grad_two, hat_two, inv_two, params[2])
    grad_mid = cot_own.astype(F32) + back_two
    x_mid = group_gather(grad_mid.astype(BF16))
    grad_out_full = dot(hidden, x_mid, ((1,), (0,)))
    grad_hidden = dot(wt_out, x_mid, ((1,), (1,)))
    grad_gate = (grad_hidden * normed_low * (sigma * (1.0 + gate * (1.0 - sigma)))).astype(BF16)
    grad_normed = (grad_hidden * swish).astype(BF16).astype(F32)
    grad_ret = (
        inv_group
        * (
            grad_normed
            - jnp.mean(grad_normed, axis=0, keepdims=True)
            - normed * jnp.mean(grad_normed * normed, axis=0, keepdims=True)
        )
    ).astype(BF16)
    grad_scores = (dot(grad_ret, values, ((0,), (0,))) * decay * scale).astype(BF16)
    grad_q = dot(keys, grad_scores, ((1,), (1,))).astype(BF16)
    grad_k = dot(query, grad_scores, ((1,), (0,))).astype(BF16)
    grad_v = dot(grad_ret, weights, ((1,), (0,))).astype(BF16)
    grad_qkv = jnp.concatenate(
        [
            grad_q.reshape(depth, -1, seq),
            grad_k.reshape(depth, -1, seq),
            grad_v.reshape(depth, -1, seq),
        ],
        axis=1,
    ).reshape(-1, seq)
    grad_one = group_reduce(
        dot(grad_qkv, all_qkv, ((0,), (0,))) + dot(grad_gate, wt_gate, ((0,), (0,)))
    )

    def from_heads(mine, count):
        send = mine.reshape(2, count, 4, part).transpose(2, 0, 1, 3).reshape(8, count, part)
        return lax.all_to_all(send, GROUP, split_axis=0, concat_axis=0, tiled=True)

    home_go = home(
        jnp.concatenate(
            [
                dot(grad_gate, x_one, ((1,), (0,))).reshape(depth, -1, width),
                grad_out_full.reshape(depth, -1, width),
            ],
            axis=1,
        ).reshape(-1, width)
    )
    home_qkv = home(dot(grad_qkv, x_one, ((1,), (0,))))
    go = from_heads(
        jnp.concatenate(
            [home_go[: 2 * kv].reshape(2, kv, width), home_go[2 * kv :].reshape(2, kv, width)],
            axis=1,
        ),
        2 * kv,
    )
    back = from_heads(
        jnp.concatenate(
            [
                home_qkv[: 2 * kq].reshape(2, kq, width),
                home_qkv[2 * kq : 4 * kq].reshape(2, kq, width),
                home_qkv[4 * kq :].reshape(2, kv, width),
            ],
            axis=1,
        ),
        2 * kq + kv,
    )

    def columns(grads, order):
        return dot(grads.reshape(-1, part), order, ((0,), (1,)))

    out_gate = columns(go[:, :kv], order_v)
    out_out = dot(order_v, go[:, kv:].reshape(-1, part), ((1,), (0,)))
    out_query = columns(back[:, :kq], order_q)
    out_key = columns(back[:, kq : 2 * kq], order_q)
    out_value = columns(back[:, 2 * kq :], order_v)
    back_one, grad_attn_gain, grad_attn_bias = layernorm_back(grad_one, hat_one, inv_one, params[0])
    grad_in = from_tokens((grad_mid + back_one).astype(BF16)).astype(F32)
    totals = lax.psum(
        jnp.stack([grad_attn_gain, grad_attn_bias, grad_ffn_gain, grad_ffn_bias]), EVERY
    )
    totals = lax.dynamic_slice_in_dim(totals, lax.axis_index(ROW) * part, part, 1)
    return (
        block_out,
        grad_in,
        out_query,
        out_key,
        out_value,
        out_gate,
        out_out,
        grad_up,
        grad_down,
        totals[0],
        totals[1],
        totals[2],
        totals[3],
    )


def solution(mesh):
    rows, cols = mesh.devices.shape
    fine = Mesh(mesh.devices.reshape(rows // 2, 2, cols // 2, 2), ("x", "k", "z", "y"))
    row, col = (("x", "k"), ("z", "y"))
    tok, unit = (P(col, row), P(row, col))
    return jax.shard_map(
        body,
        mesh=fine,
        in_specs=(tok, tok, P(row), unit, unit, unit, unit, tok, unit, tok) + (P(row),) * 4,
        out_specs=(tok, tok, unit, unit, unit, unit, tok, unit, tok) + (P(row),) * 4,
        check_vma=False,
    )
```

profile of v0, /device:TPU:0, one launch (start us, length us, event | category | flops | bytes accessed | tf_op | source)
XLA Modules:
  0.0 720.1 jit_solution(10810222214048122269)
XLA Ops:
  10.6 19.4 %all_to_all.60 = bf16[8,128,512]{2,1,0:T(8,128)(2,1)S(1)} all-to-all(bf16[8,128,512]{2,1,0:T(8,128)(2,1)S(1)} %pad_maximum_fusion.10), channel_id=1, replica_groups=mesh['x'=2,'k'=2,'z'=4,'y'=2] {'x','k','y'}, dimensions={0} | all-to-all | bytes 2097152 | tf_op jit(solution)/shard_map/all_to_all | solution.py:129
  34.4 17.0 %all_to_all.61 = bf16[8,128,512]{2,1,0:T(8,128)(2,1)S(1)} all-to-all(bf16[8,128,512]{2,1,0:T(8,128)(2,1)S(1)} %pad_maximum_fusion.12), channel_id=1, replica_groups=mesh['x'=2,'k'=2,'z'=4,'y'=2] {'x','k','y'}, dimensions={0} | all-to-all | bytes 2097152 | tf_op jit(solution)/shard_map/all_to_all | solution.py:129
  56.1 3.5 all-to-all-start
  59.7 9.8 %all_gather.19 = f32[4,2048]{1,0:T(4,128)S(1)} all-gather(f32[4,512]{1,0:T(4,128)S(1)} %pad_maximum_fusion.16), channel_id=1, replica_groups=mesh['x'=2,'k'=2,'z'=4,'y'=2] {'x','k'}, dimensions={1}, use_global_device_ids=true | all-gather | bytes 40960 | tf_op jit(solution)/shard_map/all_gather | solution.py:163
  76.5 10.8 %collective-permute-done.2 = bf16[128,2048]{1,0:T(8,128)(2,1)} collective-permute-done((bf16[128,2048]{1,0:T(8,128)(2,1)}, bf16[128,2048]{1,0:T(8,128)(2,1)}, u32[]{:S(2)}, u32[]{:S(2)}) %collective-permute-start.2) | collective-permute-done | bytes 524320 | tf_op jit(solution)/shard_map/ppermute | solution.py:22
  87.4 10.6 %collective-permute-done.1 = bf16[128,2048]{1,0:T(8,128)(2,1)} collective-permute-done((bf16[128,2048]{1,0:T(8,128)(2,1)}, bf16[128,2048]{1,0:T(8,128)(2,1)}, u32[]{:S(2)}, u32[]{:S(2)}) %collective-permute-start.1) | collective-permute-done | bytes 524320 | tf_op jit(solution)/shard_map/ppermute | solution.py:22
  99.8 5.7 all_gather.21
  110.2 3.9 all-gather.5.cloned.1.call-done
  114.1 4.7 fusion.117
  118.8 76.7 %all-gather.7.cloned.1.call-done = bf16[1024,2048]{1,0:T(8,128)(2,1)} async-done(((bf16[256,2048]{1,0:T(8,128)(2,1)}), bf16[1024,2048]{1,0:T(8,128)(2,1)}) %all-gather.7.cloned.1.call-update) | async-done | bytes 4194320 | tf_op jit(solution)/shard_map/all_gather | solution.py:155
  195.5 8.0 %convolution_convert_fusion.5 = bf16[1024,1024]{1,0:T(8,128)(2,1)S(1)} fusion(bf16[1024,2048]{1,0:T(8,128)(2,1)} %all-gather.7.cloned.1.call-done, bf16[1024,2048]{1,0:T(8,128)(2,1)} %bitcast.420), kind=kOutput, calls=%fused_computation.105 | convolution fusion | flops 4296015872 | bytes 10485760 | tf_op jit(solution)/shard_map/dot_general | solution.py:18
  203.6 2.4 fusion.6
  210.4 3.8 fusion.27
  217.0 3.9 fusion.128
  221.0 3.4 copy-done.12
  226.1 3.5 all-to-all-start.6
  230.6 3.5 fusion.16
  241.1 3.5 all-to-all-start.3
  244.7 3.0 collective-permute-start.18
  249.4 20.6 %all-to-all-done.3 = bf16[4,128,512]{2,1,0:T(8,128)(2,1)S(1)} async-done(((bf16[4,128,512]{2,1,0:T(8,128)(2,1)}), bf16[4,128,512]{2,1,0:T(8,128)(2,1)S(1)}, u32[]{:S(2)}, u32[]{:S(2)}) %all-to-all-start.3) | async-done | bytes 524320 | tf_op jit(solution)/shard_map/all_to_all | solution.py:41
  277.5 4.9 collective-permute-done.18
  283.8 8.8 %collective-permute-done.17 = bf16[128,2048]{1,0:T(8,128)(2,1)} collective-permute-done((bf16[128,2048]{1,0:T(8,128)(2,1)S(1)}, bf16[128,2048]{1,0:T(8,128)(2,1)}, u32[]{:S(2)}, u32[]{:S(2)}) %collective-permute-start.17) | collective-permute-done | bytes 524320 | tf_op jit(solution)/shard_map/ppermute | solution.py:22
  292.6 2.8 pad_maximum_fusion.7
  295.6 8.1 %collective-permute-done.9 = bf16[128,2048]{1,0:T(8,128)(2,1)S(1)} collective-permute-done((bf16[128,2048]{1,0:T(8,128)(2,1)S(1)}, bf16[128,2048]{1,0:T(8,128)(2,1)S(1)}, u32[]{:S(2)}, u32[]{:S(2)}) %collective-permute-start.9) | collective-permute-done | bytes 524320 | tf_op jit(solution)/shard_map/ppermute | solution.py:22
  304.6 10.2 %collective-permute-done.10 = bf16[128,2048]{1,0:T(8,128)(2,1)S(1)} collective-permute-done((bf16[128,2048]{1,0:T(8,128)(2,1)S(1)}, bf16[128,2048]{1,0:T(8,128)(2,1)S(1)}, u32[]{:S(2)}, u32[]{:S(2)}) %collective-permute-start.10) | collective-permute-done | bytes 524320 | tf_op jit(solution)/shard_map/ppermute | solution.py:22
  316.5 11.5 %all_to_all.62 = bf16[4,128,512]{2,1,0:T(8,128)(2,1)S(1)} all-to-all(bf16[4,128,512]{2,1,0:T(8,128)(2,1)S(1)} %bitcast.472), channel_id=1, replica_groups=mesh['x'=2,'k'=2,'z'=4,'y'=2] {'x','k'}, dimensions={0} | all-to-all | bytes 1048576 | tf_op jit(solution)/shard_map/all_to_all | solution.py:41
  329.1 4.7 pad_maximum_fusion.2
  333.8 4.6 pad_maximum_fusion.1
  338.5 10.6 %fusion.40 = (bf16[512,1024]{1,0:T(8,128)(2,1)}, f32[512,1024]{1,0:T(8,128)}, f32[1024,512]{0,1:T(8,128)}) fusion(bf16[1024,2048]{1,0:T(8,128)(2,1)} %bitcast.427, bf16[512,2048]{0,1:T(8,128)(2,1)} %all-gather.9.cloned.1.call-done), kind=kOutput, calls=%fused_computation.81 | convolution fusion | flops 2181562368 | bytes 11534336 | tf_op jit(solution)/shard_map/dot_general | solution.py:18
  349.0 23.0 %all-gather.11.cloned.1.call-done = bf16[512,2048]{0,1:T(8,128)(2,1)} async-done(((bf16[128,2048]{0,1:T(8,128)(2,1)}), bf16[512,2048]{0,1:T(8,128)(2,1)}) %all-gather.11.cloned.1.call-update) | async-done | bytes 2097168 | tf_op jit(solution)/shard_map/all_gather | solution.py:155
  372.1 7.1 fusion.37
  383.3 2.9 copy-done.11
  388.6 3.3 copy-done.9
  394.8 3.7 convolution_convert_fusion.2
  399.0 3.7 fusion.12
  411.9 17.0 %collective-permute-done.21 = bf16[128,2048]{1,0:T(8,128)(2,1)S(1)} collective-permute-done((bf16[128,2048]{1,0:T(8,128)(2,1)S(1)}, bf16[128,2048]{1,0:T(8,128)(2,1)S(1)}, u32[]{:S(2)}, u32[]{:S(2)}) %collective-permute-start.21) | collective-permute-done | bytes 524320 | tf_op jit(solution)/shard_map/ppermute | solution.py:22
  431.2 19.1 %collective-permute-done.13 = bf16[128,2048]{1,0:T(8,128)(2,1)S(1)} collective-permute-done((bf16[128,2048]{1,0:T(8,128)(2,1)S(1)}, bf16[128,2048]{1,0:T(8,128)(2,1)S(1)}, u32[]{:S(2)}, u32[]{:S(2)}) %collective-permute-start.13) | collective-permute-done | bytes 524320 | tf_op jit(solution)/shard_map/ppermute | solution.py:22
  453.6 2.6 collective-permute-start.26
  457.1 12.3 %collective-permute-done.26 = bf16[128,2048]{1,0:T(8,128)(2,1)S(1)} collective-permute-done((bf16[128,2048]{1,0:T(8,128)(2,1)S(1)}, bf16[128,2048]{1,0:T(8,128)(2,1)S(1)}, u32[]{:S(2)}, u32[]{:S(2)}) %collective-permute-start.26) | collective-permute-done | bytes 524320 | tf_op jit(solution)/shard_map/ppermute | solution.py:22
  469.4 9.3 %collective-permute-done.25 = bf16[128,2048]{1,0:T(8,128)(2,1)S(1)} collective-permute-done((bf16[128,2048]{1,0:T(8,128)(2,1)S(1)}, bf16[128,2048]{1,0:T(8,128)(2,1)S(1)}, u32[]{:S(2)}, u32[]{:S(2)}) %collective-permute-start.25) | collective-permute-done | bytes 524320 | tf_op jit(solution)/shard_map/ppermute | solution.py:22
  480.9 3.7 convolution_convert_fusion.1
  491.3 3.4 convert_reduce_fusion
  497.1 2.4 pad_maximum_fusion.4
  502.9 2.8 fusion.8
  512.3 6.0 convolution_convert_fusion
  518.4 7.3 %fusion.131 = f32[1024,2048]{1,0:T(8,128)S(1)} fusion(bf16[1024,1024]{1,0:T(8,128)(2,1)} %bitcast.444, bf16[1024,2048]{1,0:T(8,128)(2,1)} %all-gather.7.cloned.1.call-done), kind=kOutput, calls=%fused_computation.267 | convolution fusion | flops 4294967296 | bytes 14680064 | tf_op jit(solution)/shard_map/dot_general | solution.py:18
  525.7 2.5 convolution_add_fusion
  528.2 3.4 copy-done.2
  533.4 4.1 all-to-all-start.5
  537.6 8.9 %all-to-all-done.5 = bf16[4,128,512]{2,1,0:T(8,128)(2,1)} async-done(((bf16[4,128,512]{2,1,0:T(8,128)(2,1)}), bf16[4,128,512]{2,1,0:T(8,128)(2,1)}, u32[]{:S(2)}, u32[]{:S(2)}) %all-to-all-start.5) | async-done | bytes 524320 | tf_op jit(solution)/shard_map/all_to_all | solution.py:41
  550.3 4.1 all-to-all-start.10
  554.4 3.5 fusion.10
  558.0 5.4 all-to-all-done.10
  563.3 4.3 all-to-all-start.11
  574.5 2.6 copy.181
  579.2 15.4 %collective-permute-done.29 = bf16[128,2048]{1,0:T(8,128)(2,1)} collective-permute-done((bf16[128,2048]{1,0:T(8,128)(2,1)}, bf16[128,2048]{1,0:T(8,128)(2,1)}, u32[]{:S(2)}, u32[]{:S(2)}) %collective-permute-start.29) | collective-permute-done | bytes 524320 | tf_op jit(solution)/shard_map/ppermute | solution.py:22
  594.7 4.4 collective-permute-done.30
  602.6 3.5 all-to-all-start.7
  610.1 4.9 all-to-all-done.7
  614.9 3.6 all-to-all-start.9
  618.5 48.9 %psum.7 = f32[4,2048]{1,0:T(4,128)S(1)} all-reduce(f32[4,2048]{1,0:T(4,128)S(1)} %pad_maximum_fusion.15), channel_id=1, replica_groups=mesh['x'=2,'k'=2,'z'=4,'y'=2] {'x','k','z','y'}, use_global_device_ids=true, to_apply=%region_22.23 | all-reduce | flops 8192 | bytes 65536 | tf_op jit(solution)/shard_map/psum | solution.py:299
  668.1 17.8 %reduce-scatter.5.cloned.1.call-done = bf16[256,2048]{1,0:T(8,128)(2,1)} async-done(((bf16[1024,2048]{1,0:T(8,128)(2,1)}), bf16[256,2048]{1,0:T(8,128)(2,1)}) %reduce-scatter.5.cloned.1.call-update) | async-done | bytes 1048592 | tf_op jit(solution)/shard_map/reduce_scatter | solution.py:217
  689.1 3.6 all-to-all-start.8
  697.0 10.3 %all-to-all-done.8 = bf16[8,128,512]{2,1,0:T(8,128)(2,1)S(1)} async-done(((bf16[8,128,512]{2,1,0:T(8,128)(2,1)}), bf16[8,128,512]{2,1,0:T(8,128)(2,1)S(1)}, u32[]{:S(2)}, u32[]{:S(2)}) %all-to-all-start.8) | async-done | bytes 1048608 | tf_op jit(solution)/shard_map/all_to_all | solution.py:258
  (313 shorter events, 139.9 us)
Async XLA Ops:
  7.2 106.9 %all-gather.5.cloned.1.call-start = ((), (), s32[]{:S(2)}) async-start(), calls=%async_computation.16 | async-start | bytes 5242880 | tf_op jit(solution)/shard_map/all_gather | solution.py:155
  8.2 25.4 %copy-start.37 = (s32[512]{0:T(512)}, s32[512]{0:T(512)S(1)}, u32[]{:S(2)}) copy-start(s32[512]{0:T(512)S(1)} %fusion.97) | copy-start | bytes 6148
  32.9 162.7 %all-gather.7.cloned.1.call-start = ((), (), s32[]{:S(2)}) async-start(), calls=%async_computation.17 | async-start | bytes 5242880 | tf_op jit(solution)/shard_map/all_gather | solution.py:155
  56.1 13.4 %all-to-all-start = ((bf16[4,128,512]{2,1,0:T(8,128)(2,1)}), bf16[4,128,512]{2,1,0:T(8,128)(2,1)S(1)}, u32[]{:S(2)}, u32[]{:S(2)}) async-start(bf16[4,128,512]{2,1,0:T(8,128)(2,1)} %bitcast), calls=%async_computation | async-start | bytes 1048576 | tf_op jit(solution)/shard_map/all_to_all | solution.py:41
  69.5 6.8 copy-start.35
  70.0 6.3 copy-start.41
  70.3 6.0 copy-start.43
  71.4 16.0 %collective-permute-start.2 = (bf16[128,2048]{1,0:T(8,128)(2,1)}, bf16[128,2048]{1,0:T(8,128)(2,1)}, u32[]{:S(2)}, u32[]{:S(2)}) collective-permute-start(bf16[128,2048]{1,0:T(8,128)(2,1)} %add_convert_fusion.2), channel_id=1, source_target_pairs={{0,17},{1,16},{8,25},{9,24},{16,1},{17,0},{24,9},{25,8},{2,19},{3,... | collective-permute-start | bytes 1572872 | tf_op jit(solution)/shard_map/ppermute | solution.py:22
  72.6 25.4 %collective-permute-start.1 = (bf16[128,2048]{1,0:T(8,128)(2,1)}, bf16[128,2048]{1,0:T(8,128)(2,1)}, u32[]{:S(2)}, u32[]{:S(2)}) collective-permute-start(bf16[128,2048]{1,0:T(8,128)(2,1)} %add_convert_fusion.2), channel_id=1, source_target_pairs={{0,16},{1,17},{8,24},{9,25},{16,0},{17,1},{24,8},{25,9},{2,18},{3,... | collective-permute-start | bytes 1572872 | tf_op jit(solution)/shard_map/ppermute | solution.py:22
  74.3 23.7 %collective-permute-start = (bf16[128,2048]{1,0:T(8,128)(2,1)}, bf16[128,2048]{1,0:T(8,128)(2,1)}, u32[]{:S(2)}, u32[]{:S(2)}) collective-permute-start(bf16[128,2048]{1,0:T(8,128)(2,1)} %add_convert_fusion.2), channel_id=1, source_target_pairs={{0,1},{1,0},{8,9},{9,8},{16,17},{17,16},{24,25},{25,24},{2,3},{3,2... | collective-permute-start | bytes 1572872 | tf_op jit(solution)/shard_map/ppermute | solution.py:22
  99.7 6.2 collective-permute-start.3
  207.4 6.8 copy-start.5
  226.1 4.5 collective-permute-start.4
  226.1 15.0 %all-to-all-start.6 = ((bf16[4,128,512]{2,1,0:T(8,128)(2,1)}), bf16[4,128,512]{2,1,0:T(8,128)(2,1)S(1)}, u32[]{:S(2)}, u32[]{:S(2)}) async-start(bf16[4,128,512]{2,1,0:T(8,128)(2,1)} %bitcast.77), calls=%async_computation.6 | async-start | bytes 1048576 | tf_op jit(solution)/shard_map/all_to_all | solution.py:41
  236.6 34.6 %collective-permute-start.5 = (bf16[128,2048]{1,0:T(8,128)(2,1)}, bf16[128,2048]{1,0:T(8,128)(2,1)}, u32[]{:S(2)}, u32[]{:S(2)}) collective-permute-start(bf16[128,2048]{1,0:T(8,128)(2,1)} %get-tuple-element.48), channel_id=1, source_target_pairs={{0,1},{1,0},{8,9},{9,8},{16,17},{17,16},{24,25},{25,24},{2,3},{3,2... | collective-permute-start | bytes 1572872 | tf_op jit(solution)/shard_map/ppermute | solution.py:22
  238.2 34.7 %collective-permute-start.7 = (bf16[128,2048]{1,0:T(8,128)(2,1)}, bf16[128,2048]{1,0:T(8,128)(2,1)}, u32[]{:S(2)}, u32[]{:S(2)}) collective-permute-start(bf16[128,2048]{1,0:T(8,128)(2,1)} %get-tuple-element.49), channel_id=1, source_target_pairs={{0,17},{1,16},{8,25},{9,24},{16,1},{17,0},{24,9},{25,8},{2,19},{3,... | collective-permute-start | bytes 1572872 | tf_op jit(solution)/shard_map/ppermute | solution.py:22
  239.7 33.2 %collective-permute-start.6 = (bf16[128,2048]{1,0:T(8,128)(2,1)}, bf16[128,2048]{1,0:T(8,128)(2,1)}, u32[]{:S(2)}, u32[]{:S(2)}) collective-permute-start(bf16[128,2048]{1,0:T(8,128)(2,1)} %get-tuple-element.50), channel_id=1, source_target_pairs={{0,16},{1,17},{8,24},{9,25},{16,0},{17,1},{24,8},{25,9},{2,18},{3,... | collective-permute-start | bytes 1572872 | tf_op jit(solution)/shard_map/ppermute | solution.py:22
  241.1 28.8 %all-to-all-start.3 = ((bf16[4,128,512]{2,1,0:T(8,128)(2,1)}), bf16[4,128,512]{2,1,0:T(8,128)(2,1)S(1)}, u32[]{:S(2)}, u32[]{:S(2)}) async-start(bf16[4,128,512]{2,1,0:T(8,128)(2,1)} %bitcast.60), calls=%async_computation.3 | async-start | bytes 1048576 | tf_op jit(solution)/shard_map/all_to_all | solution.py:41
  244.6 93.8 %all-gather.9.cloned.1.call-start = ((), (), s32[]{:S(2)}) async-start(), calls=%async_computation.18 | async-start | bytes 2621440 | tf_op jit(solution)/shard_map/all_gather | solution.py:155
  244.7 37.6 %collective-permute-start.18 = (bf16[128,2048]{1,0:T(8,128)(2,1)S(1)}, bf16[128,2048]{1,0:T(8,128)(2,1)}, u32[]{:S(2)}, u32[]{:S(2)}) collective-permute-start(bf16[128,2048]{1,0:T(8,128)(2,1)S(1)} %bitcast.434), channel_id=1, source_target_pairs={{0,17},{1,16},{8,25},{9,24},{16,1},{17,0},{24,9},{25,8},{2,19},{3,... | collective-permute-start | bytes 1572872 | tf_op jit(solution)/shard_map/ppermute | solution.py:22
  247.7 44.9 %collective-permute-start.17 = (bf16[128,2048]{1,0:T(8,128)(2,1)S(1)}, bf16[128,2048]{1,0:T(8,128)(2,1)}, u32[]{:S(2)}, u32[]{:S(2)}) collective-permute-start(bf16[128,2048]{1,0:T(8,128)(2,1)S(1)} %bitcast.435), channel_id=1, source_target_pairs={{0,16},{1,17},{8,24},{9,25},{16,0},{17,1},{24,8},{25,9},{2,18},{3,... | collective-permute-start | bytes 1572872 | tf_op jit(solution)/shard_map/ppermute | solution.py:22
  271.0 101.1 %all-gather.11.cloned.1.call-start = ((), (), s32[]{:S(2)}) async-start(), calls=%async_computation.19 | async-start | bytes 2621440 | tf_op jit(solution)/shard_map/all_gather | solution.py:155
  271.2 21.4 %collective-permute-start.16 = (bf16[128,2048]{1,0:T(8,128)(2,1)S(1)}, bf16[128,2048]{1,0:T(8,128)(2,1)S(1)}, u32[]{:S(2)}, u32[]{:S(2)}) collective-permute-start(bf16[128,2048]{1,0:T(8,128)(2,1)S(1)} %bitcast.436), channel_id=1, source_target_pairs={{0,1},{1,0},{8,9},{9,8},{16,17},{17,16},{24,25},{25,24},{2,3},{3,2... | collective-permute-start | bytes 1572872 | tf_op jit(solution)/shard_map/ppermute | solution.py:22
  274.9 17.8 %copy-start.26 = (bf16[1,128,2048]{2,1,0:T(8,128)(2,1)S(1)}, bf16[1,128,2048]{2,1,0:T(8,128)(2,1)}, u32[]{:S(2)}) copy-start(bf16[1,128,2048]{2,1,0:T(8,128)(2,1)} %stack_reshape.3) | copy-start | bytes 1572868
  275.4 28.3 %collective-permute-start.9 = (bf16[128,2048]{1,0:T(8,128)(2,1)S(1)}, bf16[128,2048]{1,0:T(8,128)(2,1)S(1)}, u32[]{:S(2)}, u32[]{:S(2)}) collective-permute-start(bf16[128,2048]{1,0:T(8,128)(2,1)S(1)} %add_convert_fusion.1), channel_id=1, source_target_pairs={{0,16},{1,17},{8,24},{9,25},{16,0},{17,1},{24,8},{25,9},{2,18},{3,... | collective-permute-start | bytes 1572872 | tf_op jit(solution)/shard_map/ppermute | solution.py:22
  276.9 27.7 %collective-permute-start.8 = (bf16[128,2048]{1,0:T(8,128)(2,1)S(1)}, bf16[128,2048]{1,0:T(8,128)(2,1)S(1)}, u32[]{:S(2)}, u32[]{:S(2)}) collective-permute-start(bf16[128,2048]{1,0:T(8,128)(2,1)S(1)} %add_convert_fusion.1), channel_id=1, source_target_pairs={{0,1},{1,0},{8,9},{9,8},{16,17},{17,16},{24,25},{25,24},{2,3},{3,2... | collective-permute-start | bytes 1572872 | tf_op jit(solution)/shard_map/ppermute | solution.py:22
  282.3 32.5 %collective-permute-start.10 = (bf16[128,2048]{1,0:T(8,128)(2,1)S(1)}, bf16[128,2048]{1,0:T(8,128)(2,1)S(1)}, u32[]{:S(2)}, u32[]{:S(2)}) collective-permute-start(bf16[128,2048]{1,0:T(8,128)(2,1)S(1)} %add_convert_fusion.1), channel_id=1, source_target_pairs={{0,17},{1,16},{8,25},{9,24},{16,1},{17,0},{24,9},{25,8},{2,19},{3,... | collective-permute-start | bytes 1572872 | tf_op jit(solution)/shard_map/ppermute | solution.py:22
  295.4 33.7 %collective-permute-start.19 = (bf16[2,1,2,128,2048]{4,3,2,1,0:T(8,128)(2,1)}, bf16[2,1,2,128,2048]{4,3,2,1,0:T(8,128)(2,1)}, u32[]{:S(2)}, u32[]{:S(2)}) collective-permute-start(bf16[2,1,2,128,2048]{4,3,2,1,0:T(8,128)(2,1)} %bitcast.83), channel_id=1, source_target_pairs={{0,8},{1,9},{8,0},{9,1},{16,24},{17,25},{24,16},{25,17},{2,10},{3,... | collective-permute-start | bytes 6291464 | tf_op jit(solution)/shard_map/ppermute | solution.py:22
  316.5 17.3 %collective-permute-start.11 = (bf16[2,1,2,128,2048]{4,3,2,1,0:T(8,128)(2,1)}, bf16[2,1,2,128,2048]{4,3,2,1,0:T(8,128)(2,1)}, u32[]{:S(2)}, u32[]{:S(2)}) collective-permute-start(bf16[2,1,2,128,2048]{4,3,2,1,0:T(8,128)(2,1)} %bitcast.56), channel_id=1, source_target_pairs={{0,8},{1,9},{8,0},{9,1},{16,24},{17,25},{24,16},{25,17},{2,10},{3,... | collective-permute-start | bytes 6291464 | tf_op jit(solution)/shard_map/ppermute | solution.py:22
  329.0 217.4 %reduce-scatter.9.cloned.1.call-start = ((), (), s32[]{:S(2)}) async-start(), calls=%async_computation.22 | async-start | bytes 2621440 | tf_op jit(solution)/shard_map/reduce_scatter | solution.py:217
  372.1 7.1 copy-start.50
  383.3 15.7 %collective-permute-start.20 = (bf16[2,2,128,2048]{3,2,1,0:T(8,128)(2,1)}, bf16[2,2,128,2048]{3,2,1,0:T(8,128)(2,1)}, u32[]{:S(2)}, u32[]{:S(2)}) collective-permute-start(bf16[2,2,128,2048]{3,2,1,0:T(8,128)(2,1)} %fusion.30), channel_id=1, source_target_pairs={{0,8},{1,9},{8,0},{9,1},{16,24},{17,25},{24,16},{25,17},{2,10},{3,... | collective-permute-start | bytes 6291464 | tf_op jit(solution)/shard_map/ppermute | solution.py:22
  393.5 12.9 %collective-permute-start.12 = (bf16[2,2,128,2048]{3,2,1,0:T(8,128)(2,1)}, bf16[2,2,128,2048]{3,2,1,0:T(8,128)(2,1)}, u32[]{:S(2)}, u32[]{:S(2)}) collective-permute-start(bf16[2,2,128,2048]{3,2,1,0:T(8,128)(2,1)} %fusion.29), channel_id=1, source_target_pairs={{0,8},{1,9},{8,0},{9,1},{16,24},{17,25},{24,16},{25,17},{2,10},{3,... | collective-permute-start | bytes 6291464 | tf_op jit(solution)/shard_map/ppermute | solution.py:22
  398.5 149.8 %reduce-scatter.11.cloned.1.call-start = ((), (), s32[]{:S(2)}) async-start(), calls=%async_computation.23 | async-start | bytes 2621440 | tf_op jit(solution)/shard_map/reduce_scatter | solution.py:217
  399.0 7.4 %copy-start.10 = (f32[1024,2048]{1,0:T(8,128)S(1)}, f32[1024,2048]{1,0:T(8,128)}, u32[]{:S(2)}) copy-start(f32[1024,2048]{1,0:T(8,128)} %copy-done.9) | copy-start | bytes 25165828
  402.9 26.1 %collective-permute-start.21 = (bf16[128,2048]{1,0:T(8,128)(2,1)S(1)}, bf16[128,2048]{1,0:T(8,128)(2,1)S(1)}, u32[]{:S(2)}, u32[]{:S(2)}) collective-permute-start(bf16[128,2048]{1,0:T(8,128)(2,1)S(1)} %get-tuple-element.42), channel_id=1, source_target_pairs={{0,1},{1,0},{8,9},{9,8},{16,17},{17,16},{24,25},{25,24},{2,3},{3,2... | collective-permute-start | bytes 1572872 | tf_op jit(solution)/shard_map/ppermute | solution.py:22
  404.4 26.0 %collective-permute-start.23 = (bf16[128,2048]{1,0:T(8,128)(2,1)S(1)}, bf16[128,2048]{1,0:T(8,128)(2,1)S(1)}, u32[]{:S(2)}, u32[]{:S(2)}) collective-permute-start(bf16[128,2048]{1,0:T(8,128)(2,1)S(1)} %get-tuple-element.43), channel_id=1, source_target_pairs={{0,17},{1,16},{8,25},{9,24},{16,1},{17,0},{24,9},{25,8},{2,19},{3,... | collective-permute-start | bytes 1572872 | tf_op jit(solution)/shard_map/ppermute | solution.py:22
  405.9 24.6 %collective-permute-start.22 = (bf16[128,2048]{1,0:T(8,128)(2,1)S(1)}, bf16[128,2048]{1,0:T(8,128)(2,1)S(1)}, u32[]{:S(2)}, u32[]{:S(2)}) collective-permute-start(bf16[128,2048]{1,0:T(8,128)(2,1)S(1)} %get-tuple-element.44), channel_id=1, source_target_pairs={{0,16},{1,17},{8,24},{9,25},{16,0},{17,1},{24,8},{25,9},{2,18},{3,... | collective-permute-start | bytes 1572872 | tf_op jit(solution)/shard_map/ppermute | solution.py:22
  408.9 41.4 %collective-permute-start.13 = (bf16[128,2048]{1,0:T(8,128)(2,1)S(1)}, bf16[128,2048]{1,0:T(8,128)(2,1)S(1)}, u32[]{:S(2)}, u32[]{:S(2)}) collective-permute-start(bf16[128,2048]{1,0:T(8,128)(2,1)S(1)} %get-tuple-element.45), channel_id=1, source_target_pairs={{0,1},{1,0},{8,9},{9,8},{16,17},{17,16},{24,25},{25,24},{2,3},{3,2... | collective-permute-start | bytes 1572872 | tf_op jit(solution)/shard_map/ppermute | solution.py:22
  410.5 39.8 %collective-permute-start.15 = (bf16[128,2048]{1,0:T(8,128)(2,1)S(1)}, bf16[128,2048]{1,0:T(8,128)(2,1)S(1)}, u32[]{:S(2)}, u32[]{:S(2)}) collective-permute-start(bf16[128,2048]{1,0:T(8,128)(2,1)S(1)} %get-tuple-element.46), channel_id=1, source_target_pairs={{0,17},{1,16},{8,25},{9,24},{16,1},{17,0},{24,9},{25,8},{2,19},{3,... | collective-permute-start | bytes 1572872 | tf_op jit(solution)/shard_map/ppermute | solution.py:22
  429.0 22.7 %collective-permute-start.14 = (bf16[128,2048]{1,0:T(8,128)(2,1)S(1)}, bf16[128,2048]{1,0:T(8,128)(2,1)S(1)}, u32[]{:S(2)}, u32[]{:S(2)}) collective-permute-start(bf16[128,2048]{1,0:T(8,128)(2,1)S(1)} %get-tuple-element.47), channel_id=1, source_target_pairs={{0,16},{1,17},{8,24},{9,25},{16,0},{17,1},{24,8},{25,9},{2,18},{3,... | collective-permute-start | bytes 1572872 | tf_op jit(solution)/shard_map/ppermute | solution.py:22
  451.6 27.4 %copy-start.55 = (bf16[512,1024]{1,0:T(8,128)(2,1)S(1)}, bf16[512,1024]{1,0:T(8,128)(2,1)}, u32[]{:S(2)}) copy-start(bf16[512,1024]{1,0:T(8,128)(2,1)} %get-tuple-element.30) | copy-start | bytes 3145732
  453.6 15.8 %collective-permute-start.26 = (bf16[128,2048]{1,0:T(8,128)(2,1)S(1)}, bf16[128,2048]{1,0:T(8,128)(2,1)S(1)}, u32[]{:S(2)}, u32[]{:S(2)}) collective-permute-start(bf16[128,2048]{1,0:T(8,128)(2,1)S(1)} %get-tuple-element.27), channel_id=1, source_target_pairs={{0,17},{1,16},{8,25},{9,24},{16,1},{17,0},{24,9},{25,8},{2,19},{3,... | collective-permute-start | bytes 1572872 | tf_op jit(solution)/shard_map/ppermute | solution.py:22
  456.1 22.6 %collective-permute-start.25 = (bf16[128,2048]{1,0:T(8,128)(2,1)S(1)}, bf16[128,2048]{1,0:T(8,128)(2,1)S(1)}, u32[]{:S(2)}, u32[]{:S(2)}) collective-permute-start(bf16[128,2048]{1,0:T(8,128)(2,1)S(1)} %get-tuple-element.27), channel_id=1, source_target_pairs={{0,16},{1,17},{8,24},{9,25},{16,0},{17,1},{24,8},{25,9},{2,18},{3,... | collective-permute-start | bytes 1572872 | tf_op jit(solution)/shard_map/ppermute | solution.py:22
  456.7 22.0 %collective-permute-start.24 = (bf16[128,2048]{1,0:T(8,128)(2,1)S(1)}, bf16[128,2048]{1,0:T(8,128)(2,1)S(1)}, u32[]{:S(2)}, u32[]{:S(2)}) collective-permute-start(bf16[128,2048]{1,0:T(8,128)(2,1)S(1)} %get-tuple-element.27), channel_id=1, source_target_pairs={{0,1},{1,0},{8,9},{9,8},{16,17},{17,16},{24,25},{25,24},{2,3},{3,2... | collective-permute-start | bytes 1572872 | tf_op jit(solution)/shard_map/ppermute | solution.py:22
  479.0 5.7 collective-permute-start.27
  484.6 121.5 %reduce-scatter.7.cloned.1.call-start = ((), (), s32[]{:S(2)}) async-start(), calls=%async_computation.21 | async-start | bytes 5242880 | tf_op jit(solution)/shard_map/reduce_scatter | solution.py:217
  499.5 186.3 %reduce-scatter.5.cloned.1.call-start = ((), (), s32[]{:S(2)}) async-start(), calls=%async_computation.20 | async-start | bytes 5242880 | tf_op jit(solution)/shard_map/reduce_scatter | solution.py:217
  518.4 7.3 %copy-start.4 = (bf16[4,128,2048]{2,1,0:T(8,128)(2,1)S(1)}, bf16[4,128,2048]{2,1,0:T(8,128)(2,1)}, u32[]{:S(2)}) copy-start(bf16[4,128,2048]{2,1,0:T(8,128)(2,1)} %get-tuple-element.36) | copy-start | bytes 6291460
  531.9 22.5 %collective-permute-start.28 = (bf16[2,2,128,2048]{3,2,1,0:T(8,128)(2,1)S(1)}, bf16[2,2,128,2048]{3,2,1,0:T(8,128)(2,1)}, u32[]{:S(2)}, u32[]{:S(2)}) collective-permute-start(bf16[2,2,128,2048]{3,2,1,0:T(8,128)(2,1)S(1)} %fusion.31), channel_id=1, source_target_pairs={{0,8},{1,9},{8,0},{9,1},{16,24},{17,25},{24,16},{25,17},{2,10},{3,... | collective-permute-start | bytes 6291464 | tf_op jit(solution)/shard_map/ppermute | solution.py:22
  533.4 13.1 %all-to-all-start.5 = ((bf16[4,128,512]{2,1,0:T(8,128)(2,1)}), bf16[4,128,512]{2,1,0:T(8,128)(2,1)}, u32[]{:S(2)}, u32[]{:S(2)}) async-start(bf16[4,128,512]{2,1,0:T(8,128)(2,1)} %bitcast.448), calls=%async_computation.5 | async-start | bytes 1048576 | tf_op jit(solution)/shard_map/all_to_all | solution.py:41
  550.3 13.0 %all-to-all-start.10 = ((bf16[4,128,512]{2,1,0:T(8,128)(2,1)}), bf16[4,128,512]{2,1,0:T(8,128)(2,1)}, u32[]{:S(2)}, u32[]{:S(2)}) async-start(bf16[4,128,512]{2,1,0:T(8,128)(2,1)} %bitcast.450), calls=%async_computation.13 | async-start | bytes 1048576 | tf_op jit(solution)/shard_map/all_to_all | solution.py:41
  563.3 13.8 %all-to-all-start.11 = ((bf16[4,128,512]{2,1,0:T(8,128)(2,1)}), bf16[4,128,512]{2,1,0:T(8,128)(2,1)}, u32[]{:S(2)}, u32[]{:S(2)}) async-start(bf16[4,128,512]{2,1,0:T(8,128)(2,1)} %bitcast.446), calls=%async_computation.15 | async-start | bytes 1048576 | tf_op jit(solution)/shard_map/all_to_all | solution.py:41
  568.8 25.8 %collective-permute-start.29 = (bf16[128,2048]{1,0:T(8,128)(2,1)}, bf16[128,2048]{1,0:T(8,128)(2,1)}, u32[]{:S(2)}, u32[]{:S(2)}) collective-permute-start(bf16[128,2048]{1,0:T(8,128)(2,1)} %get-tuple-element.37), channel_id=1, source_target_pairs={{0,1},{1,0},{8,9},{9,8},{16,17},{17,16},{24,25},{25,24},{2,3},{3,2... | collective-permute-start | bytes 1572872 | tf_op jit(solution)/shard_map/ppermute | solution.py:22
  570.3 24.4 %collective-permute-start.31 = (bf16[128,2048]{1,0:T(8,128)(2,1)}, bf16[128,2048]{1,0:T(8,128)(2,1)}, u32[]{:S(2)}, u32[]{:S(2)}) collective-permute-start(bf16[128,2048]{1,0:T(8,128)(2,1)} %get-tuple-element.38), channel_id=1, source_target_pairs={{0,17},{1,16},{8,25},{9,24},{16,1},{17,0},{24,9},{25,8},{2,19},{3,... | collective-permute-start | bytes 1572872 | tf_op jit(solution)/shard_map/ppermute | solution.py:22
  572.3 26.8 %collective-permute-start.30 = (bf16[128,2048]{1,0:T(8,128)(2,1)}, bf16[128,2048]{1,0:T(8,128)(2,1)}, u32[]{:S(2)}, u32[]{:S(2)}) collective-permute-start(bf16[128,2048]{1,0:T(8,128)(2,1)} %get-tuple-element.39), channel_id=1, source_target_pairs={{0,16},{1,17},{8,24},{9,25},{16,0},{17,1},{24,8},{25,9},{2,18},{3,... | collective-permute-start | bytes 1572872 | tf_op jit(solution)/shard_map/ppermute | solution.py:22
  574.5 24.6 %copy-start.36 = (f32[1,2048]{1,0:T(1,128)S(1)}, f32[1,2048]{1,0:T(1,128)}, u32[]{:S(2)}) copy-start(f32[1,2048]{1,0:T(1,128)} %copy-done.35) | copy-start | bytes 24580
  574.5 24.6 %copy-start.42 = (f32[128]{0:T(128)S(1)}, f32[128]{0:T(128)}, u32[]{:S(2)}) copy-start(f32[128]{0:T(128)} %copy-done.41) | copy-start | bytes 1540
  574.5 24.6 %copy-start.44 = (f32[128]{0:T(128)S(1)}, f32[128]{0:T(128)}, u32[]{:S(2)}) copy-start(f32[128]{0:T(128)} %copy-done.43) | copy-start | bytes 1540
  579.2 22.0 %copy-start.13 = (f32[128,2048]{1,0:T(8,128)S(1)}, f32[128,2048]{1,0:T(8,128)}, u32[]{:S(2)}) copy-start(f32[128,2048]{1,0:T(8,128)} %get-tuple-element.28) | copy-start | bytes 3145732
  602.6 12.3 %all-to-all-start.7 = ((bf16[4,128,512]{2,1,0:T(8,128)(2,1)}), bf16[4,128,512]{2,1,0:T(8,128)(2,1)S(1)}, u32[]{:S(2)}, u32[]{:S(2)}) async-start(bf16[4,128,512]{2,1,0:T(8,128)(2,1)} %bitcast.395), calls=%async_computation.7 | async-start | bytes 1048576 | tf_op jit(solution)/shard_map/all_to_all | solution.py:41
  614.9 74.1 %all-to-all-start.9 = ((bf16[8,128,512]{2,1,0:T(8,128)(2,1)}), bf16[8,128,512]{2,1,0:T(8,128)(2,1)S(1)}, u32[]{:S(2)}, u32[]{:S(2)}) async-start(bf16[8,128,512]{2,1,0:T(8,128)(2,1)} %bitcast.126), calls=%async_computation.11 | async-start | bytes 2097152 | tf_op jit(solution)/shard_map/all_to_all | solution.py:258
  689.1 18.2 %all-to-all-start.8 = ((bf16[8,128,512]{2,1,0:T(8,128)(2,1)}), bf16[8,128,512]{2,1,0:T(8,128)(2,1)S(1)}, u32[]{:S(2)}, u32[]{:S(2)}) async-start(bf16[8,128,512]{2,1,0:T(8,128)(2,1)} %bitcast.116), calls=%async_computation.9 | async-start | bytes 2097152 | tf_op jit(solution)/shard_map/all_to_all | solution.py:258
  694.0 13.3 %copy-start.40 = (s32[256]{0:T(256)S(1)}, s32[256]{0:T(256)}, u32[]{:S(2)}) copy-start(s32[256]{0:T(256)} %copy-done.39) | copy-start | bytes 3076
  (44 other events, 115.1 us)
Sparse Core Ops, SparseCore 0:
  33.0 81.0 all-gather.4
  116.2 79.2 all-gather.6
  271.1 44.7 all-gather.8
  329.2 42.8 all-gather.10
  398.7 42.0 reduce-scatter.8
  484.7 41.9 reduce-scatter.10
  529.0 76.0 reduce-scatter.6
  607.5 78.3 reduce-scatter.4
where the time goes:
time: 729 us; the launch traced here: 720 us
  waiting for transfers between devices  306 us (42%)
  blocking collectives  112 us (15%)
  matrix products  89.1 us (12%)
  local copies, waits for them, and re-layouts  75 us (10%)
  starting transfers between devices  65.3 us (9%)
  other arithmetic  56.8 us (8%)
  between operations  15.7 us (2%)
    ppermute x32, waiting for transfers between devices, swap(): return lax.ppermute(value, GROUP, [(i, i ^ mask) for i in range(8)])  134 us
    all_gather x4, waiting for transfers between devices, planes(): return lax.all_gather(mine, 'z', axis=0, tiled=True)  104 us
    dot_general x31, matrix products, dot(): lax.dot_general(left, right, (over, ((), ())), preferred_element_type=F32)  89.1 us
    psum x1, blocking collectives, body(): lax.psum(jnp.stack([grad_attn_gain, grad_attn_bias, grad_ffn_gain, grad_f...  48.9 us
    all_to_all x7, waiting for transfers between devices, row_exchange(): return lax.all_to_all(parts, ROW, split_axis=0, concat_axis=0, tiled=True)  39.7 us
    all_to_all x2, blocking collectives, to_heads(): got = lax.all_to_all(send, GROUP, split_axis=0, concat_axis=0, tiled=True)  36.4 us
    unnamed x118, local copies, waits for them, and re-layouts  33.2 us
    ppermute x32, starting transfers between devices, swap(): return lax.ppermute(value, GROUP, [(i, i ^ mask) for i in range(8)])  30.5 us
  transfers between devices with their start and end apart: 49, of which 24 were waited for; matrix products, arithmetic and copies ran while one was open for 20% of the time, Pallas kernels for 0%

commit v1 on v0

--- a/solution.py
+++ b/solution.py
@@ -12,6 +12,12 @@
 EVERY = ("x", "k", "z", "y")
 F32 = jnp.float32
 BF16 = jnp.bfloat16
+
+
+def add_all(x, mesh_axis):
+    blocks = lax.all_gather(x, mesh_axis, axis=0, tiled=False)
+    acc = blocks.sum(axis=0)
+    return acc
 
 
 def dot(left, right, over):
@@ -296,7 +302,7 @@
     out_value = columns(back[:, 2 * kq :], order_v)
     back_one, grad_attn_gain, grad_attn_bias = layernorm_back(grad_one, hat_one, inv_one, params[0])
     grad_in = from_tokens((grad_mid + back_one).astype(BF16)).astype(F32)
-    totals = lax.psum(
+    totals = add_all(
         jnp.stack([grad_attn_gain, grad_attn_bias, grad_ffn_gain, grad_ffn_bias]), EVERY
     )
     totals = lax.dynamic_slice_in_dim(totals, lax.axis_index(ROW) * part, part, 1)

time: 729 us -> 771 us (1.058)
  waiting for transfers between devices: 306 us -> 404 us
  blocking collectives: 112 us -> 63.4 us
    reduce_scatter x4, waiting for transfers between devices: 17.8 us -> 73.9 us  [home(): lax.psum_scatter(full.astype(BF16), 'z', scatter_dimension=0, tiled=True)]
    all_gather x0 -> x1, waiting for transfers between devices: none -> 52.2 us  [add_all(): blocks = lax.all_gather(x, mesh_axis, axis=0, tiled=False)]
    psum x1 -> x0, blocking collectives: 48.9 us -> none  [body(): lax.psum(jnp.stack([grad_attn_gain, grad_attn_bias, grad_ffn_gain, grad_f...]
    ppermute x32, waiting for transfers between devices: 134 us -> 119 us  [swap(): return lax.ppermute(value, GROUP, [(i, i ^ mask) for i in range(8)])]
    all_to_all x7, waiting for transfers between devices: 39.7 us -> 55.4 us  [row_exchange(): return lax.all_to_all(parts, ROW, split_axis=0, concat_axis=0, tiled=True)]
    all_to_all x2, waiting for transfers between devices: 10.3 us -> 0.01 us  [from_heads(): return lax.all_to_all(send, GROUP, split_axis=0, concat_axis=0, tiled=True)]
    unnamed x118 -> x114, local copies, waits for them, and re-layouts: 33.2 us -> 29.2 us
  transfers between devices with their start and end apart: 49 -> 50, of which waited for: 24 -> 24; matrix products, arithmetic and copies ran while one was open for 20% -> 19% of each run, Pallas kernels for 0% -> 0%
where the time goes in v1:
time: 771 us; the launch traced here: 763 us
  waiting for transfers between devices  404 us (52%)
  matrix products  89.2 us (12%)
  local copies, waits for them, and re-layouts  69.7 us (9%)
  starting transfers between devices  65 us (8%)
  blocking collectives  63.4 us (8%)
  other arithmetic  56.2 us (7%)
  between operations  15.5 us (2%)
    ppermute x32, waiting for transfers between devices, swap(): return lax.ppermute(value, GROUP, [(i, i ^ mask) for i in range(8)])  119 us
    all_gather x4, waiting for transfers between devices, planes(): return lax.all_gather(mine, 'z', axis=0, tiled=True)  104 us
    dot_general x31, matrix products, dot(): lax.dot_general(left, right, (over, ((), ())), preferred_element_type=F32)  89.2 us
    reduce_scatter x4, waiting for transfers between devices, home(): lax.psum_scatter(full.astype(BF16), 'z', scatter_dimension=0, tiled=True)  73.9 us
    all_to_all x7, waiting for transfers between devices, row_exchange(): return lax.all_to_all(parts, ROW, split_axis=0, concat_axis=0, tiled=True)  55.4 us
    all_gather x1, waiting for transfers between devices, add_all(): blocks = lax.all_gather(x, mesh_axis, axis=0, tiled=False)  52.2 us
    all_to_all x2, blocking collectives, to_heads(): got = lax.all_to_all(send, GROUP, split_axis=0, concat_axis=0, tiled=True)  36.4 us
    ppermute x32, starting transfers between devices, swap(): return lax.ppermute(value, GROUP, [(i, i ^ mask) for i in range(8)])  30.5 us
  transfers between devices with their start and end apart: 50, of which 24 were waited for; matrix products, arithmetic and copies ran while one was open for 19% of the time, Pallas kernels for 0%

profile of v1, /device:TPU:0, one launch (start us, length us, event | category | flops | bytes accessed | tf_op | source)
XLA Modules:
  0.0 762.8 jit_solution(5814087555412238053)
XLA Ops:
  10.6 19.4 %all_to_all.60 = bf16[8,128,512]{2,1,0:T(8,128)(2,1)S(1)} all-to-all(bf16[8,128,512]{2,1,0:T(8,128)(2,1)S(1)} %pad_maximum_fusion.10), channel_id=1, replica_groups=mesh['x'=2,'k'=2,'z'=4,'y'=2] {'x','k','y'}, dimensions={0} | all-to-all | bytes 2097152 | tf_op jit(solution)/shard_map/all_to_all | solution.py:135
  34.4 17.0 %all_to_all.61 = bf16[8,128,512]{2,1,0:T(8,128)(2,1)S(1)} all-to-all(bf16[8,128,512]{2,1,0:T(8,128)(2,1)S(1)} %pad_maximum_fusion.12), channel_id=1, replica_groups=mesh['x'=2,'k'=2,'z'=4,'y'=2] {'x','k','y'}, dimensions={0} | all-to-all | bytes 2097152 | tf_op jit(solution)/shard_map/all_to_all | solution.py:135
  56.1 3.5 all-to-all-start
  59.7 9.8 %all_gather.25 = f32[4,2048]{1,0:T(4,128)S(1)} all-gather(f32[4,512]{1,0:T(4,128)S(1)} %pad_maximum_fusion.15), channel_id=1, replica_groups=mesh['x'=2,'k'=2,'z'=4,'y'=2] {'x','k'}, dimensions={1}, use_global_device_ids=true | all-gather | bytes 40960 | tf_op jit(solution)/shard_map/all_gather | solution.py:169
  76.5 10.8 %collective-permute-done.2 = bf16[128,2048]{1,0:T(8,128)(2,1)} collective-permute-done((bf16[128,2048]{1,0:T(8,128)(2,1)}, bf16[128,2048]{1,0:T(8,128)(2,1)}, u32[]{:S(2)}, u32[]{:S(2)}) %collective-permute-start.2) | collective-permute-done | bytes 524320 | tf_op jit(solution)/shard_map/ppermute | solution.py:28
  87.4 10.6 %collective-permute-done.1 = bf16[128,2048]{1,0:T(8,128)(2,1)} collective-permute-done((bf16[128,2048]{1,0:T(8,128)(2,1)}, bf16[128,2048]{1,0:T(8,128)(2,1)}, u32[]{:S(2)}, u32[]{:S(2)}) %collective-permute-start.1) | collective-permute-done | bytes 524320 | tf_op jit(solution)/shard_map/ppermute | solution.py:28
  99.8 5.7 all_gather.27
  110.2 3.9 all-gather.8.cloned.1.call-done
  114.1 4.7 fusion.117
  118.8 76.7 %all-gather.10.cloned.1.call-done = bf16[1024,2048]{1,0:T(8,128)(2,1)} async-done(((bf16[256,2048]{1,0:T(8,128)(2,1)}), bf16[1024,2048]{1,0:T(8,128)(2,1)}) %all-gather.10.cloned.1.call-update) | async-done | bytes 4194320 | tf_op jit(solution)/shard_map/all_gather | solution.py:161
  195.5 8.0 %convolution_convert_fusion.5 = bf16[1024,1024]{1,0:T(8,128)(2,1)S(1)} fusion(bf16[1024,2048]{1,0:T(8,128)(2,1)} %all-gather.10.cloned.1.call-done, bf16[1024,2048]{1,0:T(8,128)(2,1)} %bitcast.422), kind=kOutput, calls=%fused_computation.105 | convolution fusion | flops 4296015872 | bytes 10485760 | tf_op jit(solution)/shard_map/dot_general | solution.py:24
  203.6 2.4 fusion.6
  210.4 3.8 fusion.27
  217.0 3.9 fusion.128
  221.0 3.4 copy-done.11
  226.1 3.5 all-to-all-start.6
  230.6 3.5 fusion.16
  241.1 3.5 all-to-all-start.3
  244.7 3.0 collective-permute-start.18
  249.4 20.6 %all-to-all-done.3 = bf16[4,128,512]{2,1,0:T(8,128)(2,1)S(1)} async-done(((bf16[4,128,512]{2,1,0:T(8,128)(2,1)}), bf16[4,128,512]{2,1,0:T(8,128)(2,1)S(1)}, u32[]{:S(2)}, u32[]{:S(2)}) %all-to-all-start.3) | async-done | bytes 524320 | tf_op jit(solution)/shard_map/all_to_all | solution.py:47
  277.5 4.9 collective-permute-done.18
  283.8 8.8 %collective-permute-done.17 = bf16[128,2048]{1,0:T(8,128)(2,1)} collective-permute-done((bf16[128,2048]{1,0:T(8,128)(2,1)S(1)}, bf16[128,2048]{1,0:T(8,128)(2,1)}, u32[]{:S(2)}, u32[]{:S(2)}) %collective-permute-start.17) | collective-permute-done | bytes 524320 | tf_op jit(solution)/shard_map/ppermute | solution.py:28
  292.6 2.8 pad_maximum_fusion.7
  295.6 8.1 %collective-permute-done.9 = bf16[128,2048]{1,0:T(8,128)(2,1)S(1)} collective-permute-done((bf16[128,2048]{1,0:T(8,128)(2,1)S(1)}, bf16[128,2048]{1,0:T(8,128)(2,1)S(1)}, u32[]{:S(2)}, u32[]{:S(2)}) %collective-permute-start.9) | collective-permute-done | bytes 524320 | tf_op jit(solution)/shard_map/ppermute | solution.py:28
  304.6 10.2 %collective-permute-done.10 = bf16[128,2048]{1,0:T(8,128)(2,1)S(1)} collective-permute-done((bf16[128,2048]{1,0:T(8,128)(2,1)S(1)}, bf16[128,2048]{1,0:T(8,128)(2,1)S(1)}, u32[]{:S(2)}, u32[]{:S(2)}) %collective-permute-start.10) | collective-permute-done | bytes 524320 | tf_op jit(solution)/shard_map/ppermute | solution.py:28
  316.5 11.5 %all_to_all.62 = bf16[4,128,512]{2,1,0:T(8,128)(2,1)S(1)} all-to-all(bf16[4,128,512]{2,1,0:T(8,128)(2,1)S(1)} %bitcast.474), channel_id=1, replica_groups=mesh['x'=2,'k'=2,'z'=4,'y'=2] {'x','k'}, dimensions={0} | all-to-all | bytes 1048576 | tf_op jit(solution)/shard_map/all_to_all | solution.py:47
  329.1 4.7 pad_maximum_fusion.2
  333.8 4.6 pad_maximum_fusion.1
  338.4 10.6 %fusion.40 = (bf16[512,1024]{1,0:T(8,128)(2,1)}, f32[512,1024]{1,0:T(8,128)}, f32[1024,512]{0,1:T(8,128)}) fusion(bf16[1024,2048]{1,0:T(8,128)(2,1)} %bitcast.429, bf16[512,2048]{0,1:T(8,128)(2,1)} %all-gather.12.cloned.1.call-done), kind=kOutput, calls=%fused_computation.81 | convolution fusion | flops 2181562368 | bytes 11534336 | tf_op jit(solution)/shard_map/dot_general | solution.py:24
  349.0 23.1 %all-gather.14.cloned.1.call-done = bf16[512,2048]{0,1:T(8,128)(2,1)} async-done(((bf16[128,2048]{0,1:T(8,128)(2,1)}), bf16[512,2048]{0,1:T(8,128)(2,1)}) %all-gather.14.cloned.1.call-update) | async-done | bytes 2097168 | tf_op jit(solution)/shard_map/all_gather | solution.py:161
  372.1 7.1 fusion.37
  379.2 2.4 fusion.130
  383.3 2.9 copy-done.10
  386.2 2.4 fusion.129
  388.6 3.3 copy-done.8
  394.8 3.7 convolution_convert_fusion.2
  399.0 3.7 fusion.12
  406.4 2.4 fusion.14
  412.0 17.0 %collective-permute-done.21 = bf16[128,2048]{1,0:T(8,128)(2,1)S(1)} collective-permute-done((bf16[128,2048]{1,0:T(8,128)(2,1)S(1)}, bf16[128,2048]{1,0:T(8,128)(2,1)S(1)}, u32[]{:S(2)}, u32[]{:S(2)}) %collective-permute-start.21) | collective-permute-done | bytes 524320 | tf_op jit(solution)/shard_map/ppermute | solution.py:28
  431.2 19.1 %collective-permute-done.13 = bf16[128,2048]{1,0:T(8,128)(2,1)S(1)} collective-permute-done((bf16[128,2048]{1,0:T(8,128)(2,1)S(1)}, bf16[128,2048]{1,0:T(8,128)(2,1)S(1)}, u32[]{:S(2)}, u32[]{:S(2)}) %collective-permute-start.13) | collective-permute-done | bytes 524320 | tf_op jit(solution)/shard_map/ppermute | solution.py:28
  453.6 2.6 collective-permute-start.26
  457.1 12.3 %collective-permute-done.26 = bf16[128,2048]{1,0:T(8,128)(2,1)S(1)} collective-permute-done((bf16[128,2048]{1,0:T(8,128)(2,1)S(1)}, bf16[128,2048]{1,0:T(8,128)(2,1)S(1)}, u32[]{:S(2)}, u32[]{:S(2)}) %collective-permute-start.26) | collective-permute-done | bytes 524320 | tf_op jit(solution)/shard_map/ppermute | solution.py:28
  469.4 9.3 %collective-permute-done.25 = bf16[128,2048]{1,0:T(8,128)(2,1)S(1)} collective-permute-done((bf16[128,2048]{1,0:T(8,128)(2,1)S(1)}, bf16[128,2048]{1,0:T(8,128)(2,1)S(1)}, u32[]{:S(2)}, u32[]{:S(2)}) %collective-permute-start.25) | collective-permute-done | bytes 524320 | tf_op jit(solution)/shard_map/ppermute | solution.py:28
  480.9 3.7 convolution_convert_fusion.1
  491.4 3.4 convert_reduce_fusion
  494.8 2.4 convolution_convert_fusion.4
  502.9 2.8 fusion.8
  512.3 6.1 convolution_convert_fusion
  518.4 7.3 fusion.131
  525.7 2.5 convolution_add_fusion
  528.5 4.1 collective-permute-done.28
  538.9 4.5 all-to-all-start.5
  543.4 23.5 %all-to-all-done.5 = bf16[4,128,512]{2,1,0:T(8,128)(2,1)} async-done(((bf16[4,128,512]{2,1,0:T(8,128)(2,1)}), bf16[4,128,512]{2,1,0:T(8,128)(2,1)}, u32[]{:S(2)}, u32[]{:S(2)}) %all-to-all-start.5) | async-done | bytes 524320 | tf_op jit(solution)/shard_map/all_to_all | solution.py:47
  570.7 4.1 all-to-all-start.11
  575.0 2.8 multiply_reduce_fusion.2
  578.5 5.3 all-to-all-done.11
  583.8 3.5 all-to-all-start.10
  590.2 5.9 all-to-all-done.10
  596.1 3.5 all-to-all-start.7
  599.6 5.6 reduce-scatter.7.cloned.1.call-done
  609.1 3.6 all-to-all-start.9
  616.4 68.4 %reduce-scatter.5.cloned.1.call-done = bf16[256,2048]{1,0:T(8,128)(2,1)} async-done(((bf16[1024,2048]{1,0:T(8,128)(2,1)}), bf16[256,2048]{1,0:T(8,128)(2,1)}) %reduce-scatter.5.cloned.1.call-update) | async-done | bytes 1048592 | tf_op jit(solution)/shard_map/reduce_scatter | solution.py:223
  688.0 3.7 all-to-all-start.8
  692.8 52.2 %all-gather.16.cloned.1.call-done = f32[32,4,2048]{2,1,0:T(4,128)} async-done(((f32[1,4,2048]{2,1,0:T(4,128)}), f32[32,4,2048]{2,1,0:T(4,128)}) %all-gather.16.cloned.1.call-update) | async-done | bytes 1048592 | tf_op jit(solution)/shard_map/all_gather | solution.py:18
  (312 shorter events, 133.6 us)
Async XLA Ops:
  7.2 106.9 %all-gather.8.cloned.1.call-start = ((), (), s32[]{:S(2)}) async-start(), calls=%async_computation.16 | async-start | bytes 5242880 | tf_op jit(solution)/shard_map/all_gather | solution.py:161
  8.2 25.4 %copy-start.35 = (s32[512]{0:T(512)}, s32[512]{0:T(512)S(1)}, u32[]{:S(2)}) copy-start(s32[512]{0:T(512)S(1)} %fusion.97) | copy-start | bytes 6148
  32.9 162.7 %all-gather.10.cloned.1.call-start = ((), (), s32[]{:S(2)}) async-start(), calls=%async_computation.17 | async-start | bytes 5242880 | tf_op jit(solution)/shard_map/all_gather | solution.py:161
  56.1 13.4 %all-to-all-start = ((bf16[4,128,512]{2,1,0:T(8,128)(2,1)}), bf16[4,128,512]{2,1,0:T(8,128)(2,1)S(1)}, u32[]{:S(2)}, u32[]{:S(2)}) async-start(bf16[4,128,512]{2,1,0:T(8,128)(2,1)} %bitcast), calls=%async_computation | async-start | bytes 1048576 | tf_op jit(solution)/shard_map/all_to_all | solution.py:47
  69.5 6.8 copy-start.33
  70.0 6.3 copy-start.39
  70.3 6.0 copy-start.41
  71.4 16.0 %collective-permute-start.2 = (bf16[128,2048]{1,0:T(8,128)(2,1)}, bf16[128,2048]{1,0:T(8,128)(2,1)}, u32[]{:S(2)}, u32[]{:S(2)}) collective-permute-start(bf16[128,2048]{1,0:T(8,128)(2,1)} %add_convert_fusion.2), channel_id=1, source_target_pairs={{0,17},{1,16},{8,25},{9,24},{16,1},{17,0},{24,9},{25,8},{2,19},{3,... | collective-permute-start | bytes 1572872 | tf_op jit(solution)/shard_map/ppermute | solution.py:28
  72.6 25.4 %collective-permute-start.1 = (bf16[128,2048]{1,0:T(8,128)(2,1)}, bf16[128,2048]{1,0:T(8,128)(2,1)}, u32[]{:S(2)}, u32[]{:S(2)}) collective-permute-start(bf16[128,2048]{1,0:T(8,128)(2,1)} %add_convert_fusion.2), channel_id=1, source_target_pairs={{0,16},{1,17},{8,24},{9,25},{16,0},{17,1},{24,8},{25,9},{2,18},{3,... | collective-permute-start | bytes 1572872 | tf_op jit(solution)/shard_map/ppermute | solution.py:28
  74.3 23.7 %collective-permute-start = (bf16[128,2048]{1,0:T(8,128)(2,1)}, bf16[128,2048]{1,0:T(8,128)(2,1)}, u32[]{:S(2)}, u32[]{:S(2)}) collective-permute-start(bf16[128,2048]{1,0:T(8,128)(2,1)} %add_convert_fusion.2), channel_id=1, source_target_pairs={{0,1},{1,0},{8,9},{9,8},{16,17},{17,16},{24,25},{25,24},{2,3},{3,2... | collective-permute-start | bytes 1572872 | tf_op jit(solution)/shard_map/ppermute | solution.py:28
  99.7 6.2 collective-permute-start.3
  207.4 6.8 copy-start.4
  226.1 4.5 collective-permute-start.4
  226.1 15.0 %all-to-all-start.6 = ((bf16[4,128,512]{2,1,0:T(8,128)(2,1)}), bf16[4,128,512]{2,1,0:T(8,128)(2,1)S(1)}, u32[]{:S(2)}, u32[]{:S(2)}) async-start(bf16[4,128,512]{2,1,0:T(8,128)(2,1)} %bitcast.77), calls=%async_computation.6 | async-start | bytes 1048576 | tf_op jit(solution)/shard_map/all_to_all | solution.py:47
  236.6 34.6 %collective-permute-start.5 = (bf16[128,2048]{1,0:T(8,128)(2,1)}, bf16[128,2048]{1,0:T(8,128)(2,1)}, u32[]{:S(2)}, u32[]{:S(2)}) collective-permute-start(bf16[128,2048]{1,0:T(8,128)(2,1)} %get-tuple-element.48), channel_id=1, source_target_pairs={{0,1},{1,0},{8,9},{9,8},{16,17},{17,16},{24,25},{25,24},{2,3},{3,2... | collective-permute-start | bytes 1572872 | tf_op jit(solution)/shard_map/ppermute | solution.py:28
  238.2 34.7 %collective-permute-start.7 = (bf16[128,2048]{1,0:T(8,128)(2,1)}, bf16[128,2048]{1,0:T(8,128)(2,1)}, u32[]{:S(2)}, u32[]{:S(2)}) collective-permute-start(bf16[128,2048]{1,0:T(8,128)(2,1)} %get-tuple-element.49), channel_id=1, source_target_pairs={{0,17},{1,16},{8,25},{9,24},{16,1},{17,0},{24,9},{25,8},{2,19},{3,... | collective-permute-start | bytes 1572872 | tf_op jit(solution)/shard_map/ppermute | solution.py:28
  239.6 33.2 %collective-permute-start.6 = (bf16[128,2048]{1,0:T(8,128)(2,1)}, bf16[128,2048]{1,0:T(8,128)(2,1)}, u32[]{:S(2)}, u32[]{:S(2)}) collective-permute-start(bf16[128,2048]{1,0:T(8,128)(2,1)} %get-tuple-element.50), channel_id=1, source_target_pairs={{0,16},{1,17},{8,24},{9,25},{16,0},{17,1},{24,8},{25,9},{2,18},{3,... | collective-permute-start | bytes 1572872 | tf_op jit(solution)/shard_map/ppermute | solution.py:28
  241.1 28.8 %all-to-all-start.3 = ((bf16[4,128,512]{2,1,0:T(8,128)(2,1)}), bf16[4,128,512]{2,1,0:T(8,128)(2,1)S(1)}, u32[]{:S(2)}, u32[]{:S(2)}) async-start(bf16[4,128,512]{2,1,0:T(8,128)(2,1)} %bitcast.60), calls=%async_computation.3 | async-start | bytes 1048576 | tf_op jit(solution)/shard_map/all_to_all | solution.py:47
  244.6 93.8 %all-gather.12.cloned.1.call-start = ((), (), s32[]{:S(2)}) async-start(), calls=%async_computation.18 | async-start | bytes 2621440 | tf_op jit(solution)/shard_map/all_gather | solution.py:161
  244.7 37.6 %collective-permute-start.18 = (bf16[128,2048]{1,0:T(8,128)(2,1)S(1)}, bf16[128,2048]{1,0:T(8,128)(2,1)}, u32[]{:S(2)}, u32[]{:S(2)}) collective-permute-start(bf16[128,2048]{1,0:T(8,128)(2,1)S(1)} %bitcast.436), channel_id=1, source_target_pairs={{0,17},{1,16},{8,25},{9,24},{16,1},{17,0},{24,9},{25,8},{2,19},{3,... | collective-permute-start | bytes 1572872 | tf_op jit(solution)/shard_map/ppermute | solution.py:28
  247.7 44.9 %collective-permute-start.17 = (bf16[128,2048]{1,0:T(8,128)(2,1)S(1)}, bf16[128,2048]{1,0:T(8,128)(2,1)}, u32[]{:S(2)}, u32[]{:S(2)}) collective-permute-start(bf16[128,2048]{1,0:T(8,128)(2,1)S(1)} %bitcast.437), channel_id=1, source_target_pairs={{0,16},{1,17},{8,24},{9,25},{16,0},{17,1},{24,8},{25,9},{2,18},{3,... | collective-permute-start | bytes 1572872 | tf_op jit(solution)/shard_map/ppermute | solution.py:28
  271.0 101.1 %all-gather.14.cloned.1.call-start = ((), (), s32[]{:S(2)}) async-start(), calls=%async_computation.19 | async-start | bytes 2621440 | tf_op jit(solution)/shard_map/all_gather | solution.py:161
  271.2 21.4 %collective-permute-start.16 = (bf16[128,2048]{1,0:T(8,128)(2,1)S(1)}, bf16[128,2048]{1,0:T(8,128)(2,1)S(1)}, u32[]{:S(2)}, u32[]{:S(2)}) collective-permute-start(bf16[128,2048]{1,0:T(8,128)(2,1)S(1)} %bitcast.438), channel_id=1, source_target_pairs={{0,1},{1,0},{8,9},{9,8},{16,17},{17,16},{24,25},{25,24},{2,3},{3,2... | collective-permute-start | bytes 1572872 | tf_op jit(solution)/shard_map/ppermute | solution.py:28
  274.8 17.8 %copy-start.24 = (bf16[1,128,2048]{2,1,0:T(8,128)(2,1)S(1)}, bf16[1,128,2048]{2,1,0:T(8,128)(2,1)}, u32[]{:S(2)}) copy-start(bf16[1,128,2048]{2,1,0:T(8,128)(2,1)} %stack_reshape.3) | copy-start | bytes 1572868
  275.4 28.3 %collective-permute-start.9 = (bf16[128,2048]{1,0:T(8,128)(2,1)S(1)}, bf16[128,2048]{1,0:T(8,128)(2,1)S(1)}, u32[]{:S(2)}, u32[]{:S(2)}) collective-permute-start(bf16[128,2048]{1,0:T(8,128)(2,1)S(1)} %add_convert_fusion.1), channel_id=1, source_target_pairs={{0,16},{1,17},{8,24},{9,25},{16,0},{17,1},{24,8},{25,9},{2,18},{3,... | collective-permute-start | bytes 1572872 | tf_op jit(solution)/shard_map/ppermute | solution.py:28
  276.9 27.7 %collective-permute-start.8 = (bf16[128,2048]{1,0:T(8,128)(2,1)S(1)}, bf16[128,2048]{1,0:T(8,128)(2,1)S(1)}, u32[]{:S(2)}, u32[]{:S(2)}) collective-permute-start(bf16[128,2048]{1,0:T(8,128)(2,1)S(1)} %add_convert_fusion.1), channel_id=1, source_target_pairs={{0,1},{1,0},{8,9},{9,8},{16,17},{17,16},{24,25},{25,24},{2,3},{3,2... | collective-permute-start | bytes 1572872 | tf_op jit(solution)/shard_map/ppermute | solution.py:28
  282.3 32.5 %collective-permute-start.10 = (bf16[128,2048]{1,0:T(8,128)(2,1)S(1)}, bf16[128,2048]{1,0:T(8,128)(2,1)S(1)}, u32[]{:S(2)}, u32[]{:S(2)}) collective-permute-start(bf16[128,2048]{1,0:T(8,128)(2,1)S(1)} %add_convert_fusion.1), channel_id=1, source_target_pairs={{0,17},{1,16},{8,25},{9,24},{16,1},{17,0},{24,9},{25,8},{2,19},{3,... | collective-permute-start | bytes 1572872 | tf_op jit(solution)/shard_map/ppermute | solution.py:28
  295.4 33.7 %collective-permute-start.19 = (bf16[2,1,2,128,2048]{4,3,2,1,0:T(8,128)(2,1)}, bf16[2,1,2,128,2048]{4,3,2,1,0:T(8,128)(2,1)}, u32[]{:S(2)}, u32[]{:S(2)}) collective-permute-start(bf16[2,1,2,128,2048]{4,3,2,1,0:T(8,128)(2,1)} %bitcast.83), channel_id=1, source_target_pairs={{0,8},{1,9},{8,0},{9,1},{16,24},{17,25},{24,16},{25,17},{2,10},{3,... | collective-permute-start | bytes 6291464 | tf_op jit(solution)/shard_map/ppermute | solution.py:28
  316.5 17.3 %collective-permute-start.11 = (bf16[2,1,2,128,2048]{4,3,2,1,0:T(8,128)(2,1)}, bf16[2,1,2,128,2048]{4,3,2,1,0:T(8,128)(2,1)}, u32[]{:S(2)}, u32[]{:S(2)}) collective-permute-start(bf16[2,1,2,128,2048]{4,3,2,1,0:T(8,128)(2,1)} %bitcast.56), channel_id=1, source_target_pairs={{0,8},{1,9},{8,0},{9,1},{16,24},{17,25},{24,16},{25,17},{2,10},{3,... | collective-permute-start | bytes 6291464 | tf_op jit(solution)/shard_map/ppermute | solution.py:28
  329.0 237.9 %reduce-scatter.9.cloned.1.call-start = ((), (), s32[]{:S(2)}) async-start(), calls=%async_computation.22 | async-start | bytes 2621440 | tf_op jit(solution)/shard_map/reduce_scatter | solution.py:223
  372.1 7.1 copy-start.48
  383.3 15.7 %collective-permute-start.20 = (bf16[2,2,128,2048]{3,2,1,0:T(8,128)(2,1)}, bf16[2,2,128,2048]{3,2,1,0:T(8,128)(2,1)}, u32[]{:S(2)}, u32[]{:S(2)}) collective-permute-start(bf16[2,2,128,2048]{3,2,1,0:T(8,128)(2,1)} %fusion.30), channel_id=1, source_target_pairs={{0,8},{1,9},{8,0},{9,1},{16,24},{17,25},{24,16},{25,17},{2,10},{3,... | collective-permute-start | bytes 6291464 | tf_op jit(solution)/shard_map/ppermute | solution.py:28
  393.5 12.9 %collective-permute-start.12 = (bf16[2,2,128,2048]{3,2,1,0:T(8,128)(2,1)}, bf16[2,2,128,2048]{3,2,1,0:T(8,128)(2,1)}, u32[]{:S(2)}, u32[]{:S(2)}) collective-permute-start(bf16[2,2,128,2048]{3,2,1,0:T(8,128)(2,1)} %fusion.29), channel_id=1, source_target_pairs={{0,8},{1,9},{8,0},{9,1},{16,24},{17,25},{24,16},{25,17},{2,10},{3,... | collective-permute-start | bytes 6291464 | tf_op jit(solution)/shard_map/ppermute | solution.py:28
  398.5 170.3 %reduce-scatter.11.cloned.1.call-start = ((), (), s32[]{:S(2)}) async-start(), calls=%async_computation.23 | async-start | bytes 2621440 | tf_op jit(solution)/shard_map/reduce_scatter | solution.py:223
  399.0 7.4 copy-start.9
  402.9 26.1 %collective-permute-start.21 = (bf16[128,2048]{1,0:T(8,128)(2,1)S(1)}, bf16[128,2048]{1,0:T(8,128)(2,1)S(1)}, u32[]{:S(2)}, u32[]{:S(2)}) collective-permute-start(bf16[128,2048]{1,0:T(8,128)(2,1)S(1)} %get-tuple-element.42), channel_id=1, source_target_pairs={{0,1},{1,0},{8,9},{9,8},{16,17},{17,16},{24,25},{25,24},{2,3},{3,2... | collective-permute-start | bytes 1572872 | tf_op jit(solution)/shard_map/ppermute | solution.py:28
  404.4 26.0 %collective-permute-start.23 = (bf16[128,2048]{1,0:T(8,128)(2,1)S(1)}, bf16[128,2048]{1,0:T(8,128)(2,1)S(1)}, u32[]{:S(2)}, u32[]{:S(2)}) collective-permute-start(bf16[128,2048]{1,0:T(8,128)(2,1)S(1)} %get-tuple-element.43), channel_id=1, source_target_pairs={{0,17},{1,16},{8,25},{9,24},{16,1},{17,0},{24,9},{25,8},{2,19},{3,... | collective-permute-start | bytes 1572872 | tf_op jit(solution)/shard_map/ppermute | solution.py:28
  405.9 24.6 %collective-permute-start.22 = (bf16[128,2048]{1,0:T(8,128)(2,1)S(1)}, bf16[128,2048]{1,0:T(8,128)(2,1)S(1)}, u32[]{:S(2)}, u32[]{:S(2)}) collective-permute-start(bf16[128,2048]{1,0:T(8,128)(2,1)S(1)} %get-tuple-element.44), channel_id=1, source_target_pairs={{0,16},{1,17},{8,24},{9,25},{16,0},{17,1},{24,8},{25,9},{2,18},{3,... | collective-permute-start | bytes 1572872 | tf_op jit(solution)/shard_map/ppermute | solution.py:28
  408.9 41.4 %collective-permute-start.13 = (bf16[128,2048]{1,0:T(8,128)(2,1)S(1)}, bf16[128,2048]{1,0:T(8,128)(2,1)S(1)}, u32[]{:S(2)}, u32[]{:S(2)}) collective-permute-start(bf16[128,2048]{1,0:T(8,128)(2,1)S(1)} %get-tuple-element.45), channel_id=1, source_target_pairs={{0,1},{1,0},{8,9},{9,8},{16,17},{17,16},{24,25},{25,24},{2,3},{3,2... | collective-permute-start | bytes 1572872 | tf_op jit(solution)/shard_map/ppermute | solution.py:28
  410.5 39.8 %collective-permute-start.15 = (bf16[128,2048]{1,0:T(8,128)(2,1)S(1)}, bf16[128,2048]{1,0:T(8,128)(2,1)S(1)}, u32[]{:S(2)}, u32[]{:S(2)}) collective-permute-start(bf16[128,2048]{1,0:T(8,128)(2,1)S(1)} %get-tuple-element.46), channel_id=1, source_target_pairs={{0,17},{1,16},{8,25},{9,24},{16,1},{17,0},{24,9},{25,8},{2,19},{3,... | collective-permute-start | bytes 1572872 | tf_op jit(solution)/shard_map/ppermute | solution.py:28
  429.0 22.7 %collective-permute-start.14 = (bf16[128,2048]{1,0:T(8,128)(2,1)S(1)}, bf16[128,2048]{1,0:T(8,128)(2,1)S(1)}, u32[]{:S(2)}, u32[]{:S(2)}) collective-permute-start(bf16[128,2048]{1,0:T(8,128)(2,1)S(1)} %get-tuple-element.47), channel_id=1, source_target_pairs={{0,16},{1,17},{8,24},{9,25},{16,0},{17,1},{24,8},{25,9},{2,18},{3,... | collective-permute-start | bytes 1572872 | tf_op jit(solution)/shard_map/ppermute | solution.py:28
  451.6 27.4 %copy-start.53 = (bf16[512,1024]{1,0:T(8,128)(2,1)S(1)}, bf16[512,1024]{1,0:T(8,128)(2,1)}, u32[]{:S(2)}) copy-start(bf16[512,1024]{1,0:T(8,128)(2,1)} %get-tuple-element.30) | copy-start | bytes 3145732
  453.6 15.8 %collective-permute-start.26 = (bf16[128,2048]{1,0:T(8,128)(2,1)S(1)}, bf16[128,2048]{1,0:T(8,128)(2,1)S(1)}, u32[]{:S(2)}, u32[]{:S(2)}) collective-permute-start(bf16[128,2048]{1,0:T(8,128)(2,1)S(1)} %get-tuple-element.27), channel_id=1, source_target_pairs={{0,17},{1,16},{8,25},{9,24},{16,1},{17,0},{24,9},{25,8},{2,19},{3,... | collective-permute-start | bytes 1572872 | tf_op jit(solution)/shard_map/ppermute | solution.py:28
  456.2 22.6 %collective-permute-start.25 = (bf16[128,2048]{1,0:T(8,128)(2,1)S(1)}, bf16[128,2048]{1,0:T(8,128)(2,1)S(1)}, u32[]{:S(2)}, u32[]{:S(2)}) collective-permute-start(bf16[128,2048]{1,0:T(8,128)(2,1)S(1)} %get-tuple-element.27), channel_id=1, source_target_pairs={{0,16},{1,17},{8,24},{9,25},{16,0},{17,1},{24,8},{25,9},{2,18},{3,... | collective-permute-start | bytes 1572872 | tf_op jit(solution)/shard_map/ppermute | solution.py:28
  456.7 22.0 %collective-permute-start.24 = (bf16[128,2048]{1,0:T(8,128)(2,1)S(1)}, bf16[128,2048]{1,0:T(8,128)(2,1)S(1)}, u32[]{:S(2)}, u32[]{:S(2)}) collective-permute-start(bf16[128,2048]{1,0:T(8,128)(2,1)S(1)} %get-tuple-element.27), channel_id=1, source_target_pairs={{0,1},{1,0},{8,9},{9,8},{16,17},{17,16},{24,25},{25,24},{2,3},{3,2... | collective-permute-start | bytes 1572872 | tf_op jit(solution)/shard_map/ppermute | solution.py:28
  479.0 5.7 collective-permute-start.27
  484.6 120.5 %reduce-scatter.7.cloned.1.call-start = ((), (), s32[]{:S(2)}) async-start(), calls=%async_computation.21 | async-start | bytes 5242880 | tf_op jit(solution)/shard_map/reduce_scatter | solution.py:223
  499.5 185.3 %reduce-scatter.5.cloned.1.call-start = ((), (), s32[]{:S(2)}) async-start(), calls=%async_computation.20 | async-start | bytes 5242880 | tf_op jit(solution)/shard_map/reduce_scatter | solution.py:223
  518.4 7.3 copy-start.3
  528.5 4.2 collective-permute-start.28
  534.6 40.3 %collective-permute-start.29 = (bf16[128,2048]{1,0:T(8,128)(2,1)}, bf16[128,2048]{1,0:T(8,128)(2,1)}, u32[]{:S(2)}, u32[]{:S(2)}) collective-permute-start(bf16[128,2048]{1,0:T(8,128)(2,1)} %get-tuple-element.37), channel_id=1, source_target_pairs={{0,1},{1,0},{8,9},{9,8},{16,17},{17,16},{24,25},{25,24},{2,3},{3,2... | collective-permute-start | bytes 1572872 | tf_op jit(solution)/shard_map/ppermute | solution.py:28
  536.0 38.9 %collective-permute-start.31 = (bf16[128,2048]{1,0:T(8,128)(2,1)}, bf16[128,2048]{1,0:T(8,128)(2,1)}, u32[]{:S(2)}, u32[]{:S(2)}) collective-permute-start(bf16[128,2048]{1,0:T(8,128)(2,1)} %get-tuple-element.38), channel_id=1, source_target_pairs={{0,17},{1,16},{8,25},{9,24},{16,1},{17,0},{24,9},{25,8},{2,19},{3,... | collective-permute-start | bytes 1572872 | tf_op jit(solution)/shard_map/ppermute | solution.py:28
  537.6 37.4 %collective-permute-start.30 = (bf16[128,2048]{1,0:T(8,128)(2,1)}, bf16[128,2048]{1,0:T(8,128)(2,1)}, u32[]{:S(2)}, u32[]{:S(2)}) collective-permute-start(bf16[128,2048]{1,0:T(8,128)(2,1)} %get-tuple-element.39), channel_id=1, source_target_pairs={{0,16},{1,17},{8,24},{9,25},{16,0},{17,1},{24,8},{25,9},{2,18},{3,... | collective-permute-start | bytes 1572872 | tf_op jit(solution)/shard_map/ppermute | solution.py:28
  538.9 36.1 %copy-start.34 = (f32[1,2048]{1,0:T(1,128)S(1)}, f32[1,2048]{1,0:T(1,128)}, u32[]{:S(2)}) copy-start(f32[1,2048]{1,0:T(1,128)} %copy-done.33) | copy-start | bytes 24580
  538.9 36.1 %copy-start.40 = (f32[128]{0:T(128)S(1)}, f32[128]{0:T(128)}, u32[]{:S(2)}) copy-start(f32[128]{0:T(128)} %copy-done.39) | copy-start | bytes 1540
  538.9 36.1 %copy-start.42 = (f32[128]{0:T(128)S(1)}, f32[128]{0:T(128)}, u32[]{:S(2)}) copy-start(f32[128]{0:T(128)} %copy-done.41) | copy-start | bytes 1540
  538.9 28.0 %all-to-all-start.5 = ((bf16[4,128,512]{2,1,0:T(8,128)(2,1)}), bf16[4,128,512]{2,1,0:T(8,128)(2,1)}, u32[]{:S(2)}, u32[]{:S(2)}) async-start(bf16[4,128,512]{2,1,0:T(8,128)(2,1)} %bitcast.451), calls=%async_computation.5 | async-start | bytes 1048576 | tf_op jit(solution)/shard_map/all_to_all | solution.py:47
  570.7 13.1 %all-to-all-start.11 = ((bf16[4,128,512]{2,1,0:T(8,128)(2,1)}), bf16[4,128,512]{2,1,0:T(8,128)(2,1)}, u32[]{:S(2)}, u32[]{:S(2)}) async-start(bf16[4,128,512]{2,1,0:T(8,128)(2,1)} %bitcast.449), calls=%async_computation.15 | async-start | bytes 1048576 | tf_op jit(solution)/shard_map/all_to_all | solution.py:47
  574.9 170.1 %all-gather.16.cloned.1.call-start = ((), (), s32[]{:S(2)}) async-start(), calls=%async_computation.24 | async-start | bytes 1081344 | tf_op jit(solution)/shard_map/all_gather | solution.py:18
  583.8 12.3 %all-to-all-start.10 = ((bf16[4,128,512]{2,1,0:T(8,128)(2,1)}), bf16[4,128,512]{2,1,0:T(8,128)(2,1)S(1)}, u32[]{:S(2)}, u32[]{:S(2)}) async-start(bf16[4,128,512]{2,1,0:T(8,128)(2,1)} %bitcast.448), calls=%async_computation.13 | async-start | bytes 1048576 | tf_op jit(solution)/shard_map/all_to_all | solution.py:47
  596.1 13.0 %all-to-all-start.7 = ((bf16[4,128,512]{2,1,0:T(8,128)(2,1)}), bf16[4,128,512]{2,1,0:T(8,128)(2,1)S(1)}, u32[]{:S(2)}, u32[]{:S(2)}) async-start(bf16[4,128,512]{2,1,0:T(8,128)(2,1)} %bitcast.397), calls=%async_computation.7 | async-start | bytes 1048576 | tf_op jit(solution)/shard_map/all_to_all | solution.py:47
  609.1 78.9 %all-to-all-start.9 = ((bf16[8,128,512]{2,1,0:T(8,128)(2,1)}), bf16[8,128,512]{2,1,0:T(8,128)(2,1)S(1)}, u32[]{:S(2)}, u32[]{:S(2)}) async-start(bf16[8,128,512]{2,1,0:T(8,128)(2,1)} %bitcast.126), calls=%async_computation.11 | async-start | bytes 2097152 | tf_op jit(solution)/shard_map/all_to_all | solution.py:264
  688.0 62.2 %all-to-all-start.8 = ((bf16[8,128,512]{2,1,0:T(8,128)(2,1)}), bf16[8,128,512]{2,1,0:T(8,128)(2,1)S(1)}, u32[]{:S(2)}, u32[]{:S(2)}) async-start(bf16[8,128,512]{2,1,0:T(8,128)(2,1)} %bitcast.116), calls=%async_computation.9 | async-start | bytes 2097152 | tf_op jit(solution)/shard_map/all_to_all | solution.py:264
  691.7 55.5 %copy-start.36 = (s32[512]{0:T(512)S(1)}, s32[512]{0:T(512)}, u32[]{:S(2)}) copy-start(s32[512]{0:T(512)} %copy-done.35) | copy-start | bytes 6148
  (43 other events, 117.2 us)
Sparse Core Ops, SparseCore 0:
  33.0 81.0 all-gather.7
  116.2 79.2 all-gather.9
  271.1 44.7 all-gather.11
  329.1 42.8 all-gather.13
  398.7 42.0 reduce-scatter.8
  484.7 41.8 reduce-scatter.10
  528.9 76.1 reduce-scatter.6
  607.5 77.2 reduce-scatter.4
  688.5 56.4 all-gather.15
